TPU v7x, 32 devices: a whole 2x2x4 slice. The times are simulated.
32 devices in a mesh: gx: 4 (over z), yz: 8 (over y, x, core).
Axes of the slice: x: 2, y: 2, z: 4, core: 2. Of those that a mesh axis runs over, the one named last changes fastest.
Arguments:
- camera_accel: float32 [4, 1024, 3, 16, 128], P('gx', 'yz'), may hold values from -8 to 8
- camera_weight: float32 [4, 1024, 16, 128], P('gx', 'yz'), may hold values from 0.25 to 4
- brick_slot: int32 [4, 1024], P('gx', 'yz'), may hold values from 0 to 1023, as said below
- brick_solid: int32 [4, 1024], P('gx', 'yz'), may hold values from 0 to 1, as said below
Outputs:
- solution: float32 [8, 1024, 1024], P('yz', 'gx')
- residual: float32 [8, 1024, 1024], P('yz', 'gx')
Inputs may be any that keep to these rules, and one draw needn't show every extreme that they name: `brick_slot`: row g lists each in-slab brick number of slab g once; entries j * 128 to (j + 1) * 128 - 1 are the bricks that camera owner j holds; brick number i belongs to solver owner i // 128. One camera owner holds at most 24 bricks of one solver owner, and exactly 24 of some in every slab. `brick_solid`: 1 marks a solid brick, numbered as in brick_slot; every slab has solid and fluid bricks.
All inputs are finite; a program needn't handle non-finite values.
Results may differ from a plain program's by a relative error of at most 0.00024.
Values sent between devices are 32-bit elements; how exact they have to be, the bound alone decides.
A program may use at most 128 MiB of HBM per device.

v0:
```python
import jax
import jax.numpy as jnp
from jax import lax
from jax.sharding import PartitionSpec as P

NX = 1024
NY = 1024
BR = 16
B = 128
ITERS = 2


shift_rate = 0.05
spectral_gain = 1.0
spectral_floor = 2.0
highest = lax.Precision.HIGHEST


def padded_2(block, sides, width):
    for axis, dim in sides:
        count = lax.axis_size(axis)
        forward = [(i, i + 1) for i in range(count - 1)]
        backward = [(target, source) for source, target in forward]
        low = lax.ppermute(
            lax.slice_in_dim(block, block.shape[dim] - width, None, axis=dim), axis, forward
        )
        high = lax.ppermute(lax.slice_in_dim(block, 0, width, axis=dim), axis, backward)
        block = jnp.concatenate([low, block, high], axis=dim)
    return block


def cosine_table(length, row_count, col_count):
    row_ids = jnp.arange(row_count, dtype=jnp.int32)
    col_ids = jnp.arange(col_count, dtype=jnp.int32)
    phases = jnp.remainder(row_ids[:, None] * (2 * col_ids[None, :] + 1), 4 * length).astype(
        jnp.float32
    )
    angles = phases * (jnp.pi / (2.0 * length))
    norm_scale = jnp.where(row_ids == 0, 1.0 / length, 2.0 / length).astype(jnp.float32)
    return jnp.sqrt(norm_scale)[:, None] * jnp.cos(angles)


def eigen_values(length, first_mode, mode_count):
    modes = (first_mode + jnp.arange(mode_count, dtype=jnp.int32)).astype(jnp.float32)
    return 2.0 - 2.0 * jnp.cos(modes * (jnp.pi / length))


def to_block(bricks, x_bricks, y_bricks, z_cells, x_rows):
    channels = bricks.shape[1]
    col_cells = bricks.shape[3]
    shaped = bricks.reshape(x_bricks, y_bricks, channels, z_cells, x_rows, col_cells)
    shaped = jnp.transpose(shaped, (2, 3, 0, 4, 1, 5))
    return shaped.reshape(channels, z_cells, x_bricks * x_rows, y_bricks * col_cells)


def operate(values_in, coefs):
    face_z, face_x, face_y, diagonal = coefs
    padded = padded_2(values_in, (("gx", 1), ("yz", 0)), 1)
    nearby = face_z[:-1] * padded[:-2, 1:-1] + face_z[1:] * padded[2:, 1:-1]
    nearby = nearby + face_x[:, :-1] * padded[1:-1, :-2] + face_x[:, 1:] * padded[1:-1, 2:]
    nearby = (
        nearby
        + face_y * jnp.roll(values_in, -1, 2)
        + jnp.roll(face_y, 1, 2) * jnp.roll(values_in, 1, 2)
    )
    return diagonal * values_in - nearby


def precondition(residual, fluid_cells, table_y, table_x):
    y_cells = residual.shape[2]
    spectrum = jnp.einsum("zxy,ky->zxk", residual, table_y, precision=highest)
    pencil = lax.all_to_all(spectrum, "gx", split_axis=2, concat_axis=1, tiled=True)
    y_part = pencil.shape[2]
    first_y = lax.axis_index("gx") * y_part
    denom = (
        spectral_gain
        * (eigen_values(NX, 0, NX)[:, None] + eigen_values(y_cells, first_y, y_part)[None, :])
        + spectral_floor
    )
    modes = jnp.einsum("kx,zxy->zky", table_x, pencil, precision=highest) / denom[None]
    spatial = jnp.einsum("kx,zky->zxy", table_x, modes, precision=highest)
    mixed = lax.all_to_all(spatial, "gx", split_axis=1, concat_axis=2, tiled=True)
    spatial_out = jnp.einsum("zxk,ky->zxy", mixed, table_y, precision=highest)
    return fluid_cells * spatial_out


def paired(residual, update, image_of):
    return lax.psum((jnp.sum(residual * update), jnp.sum(image_of * update)), ("gx", "yz"))


def on_device(camera_accel, camera_weight, brick_slot, brick_solid):
    owner_count = lax.axis_size("yz")
    slot_count = brick_slot.shape[1]
    per_owner = 3 * slot_count // (2 * owner_count)
    row_cells = camera_weight.shape[2]
    col_cells = camera_weight.shape[3]
    z_cells = row_cells // BR
    x_bricks = NX // lax.axis_size("gx") // BR
    y_bricks = NY // B
    brick_ids = brick_slot[0]
    owners_of = brick_ids // slot_count
    owner_ids = jnp.arange(owner_count, dtype=jnp.int32)
    one_hot = (owners_of[:, None] == owner_ids[None, :]).astype(jnp.int32)
    earlier = jnp.cumsum(one_hot, axis=0) - one_hot
    target = owners_of * per_owner + jnp.sum(earlier * one_hot, axis=1)
    positions = jnp.arange(owner_count * per_owner, dtype=jnp.int32)
    matches = target[None, :] == positions[:, None]
    filled = jnp.any(matches, axis=1)
    source = jnp.sum(
        jnp.where(matches, jnp.arange(slot_count, dtype=jnp.int32)[None, :], 0), axis=1
    )
    send_ids = jnp.where(filled, brick_ids[source] % slot_count, -1).reshape(owner_count, per_owner)
    send_accel = jnp.where(filled[:, None, None, None], camera_accel[0][source], 0.0)
    send_accel = send_accel.reshape(owner_count, per_owner, 3, row_cells, col_cells)
    send_weight = jnp.where(filled[:, None, None], camera_weight[0][source], 0.0)
    send_weight = send_weight.reshape(owner_count, per_owner, row_cells, col_cells)
    recv_ids, recv_accel, recv_weight = (
        lax.all_to_all(send_ids, "yz", split_axis=0, concat_axis=0, tiled=True),
        lax.all_to_all(send_accel, "yz", split_axis=0, concat_axis=0, tiled=True),
        lax.all_to_all(send_weight, "yz", split_axis=0, concat_axis=0, tiled=True),
    )
    flat_ids = recv_ids.reshape(-1)
    wanted = jnp.arange(slot_count, dtype=jnp.int32)
    arrived = flat_ids[None, :] == wanted[:, None]
    anchor = jnp.sum(
        jnp.where(arrived, jnp.arange(flat_ids.shape[0], dtype=jnp.int32)[None, :], 0), axis=1
    )
    fluid_bricks = (1 - brick_solid[0]).astype(jnp.float32)
    accel_bricks = recv_accel.reshape(-1, 3, row_cells, col_cells)[anchor]
    weight_bricks = recv_weight.reshape(-1, 1, row_cells, col_cells)[anchor]
    payload = (
        jnp.concatenate([accel_bricks, weight_bricks], axis=1) * fluid_bricks[:, None, None, None]
    )
    fields = to_block(payload, x_bricks, y_bricks, z_cells, BR)
    fluid_tiles = jnp.broadcast_to(
        fluid_bricks[:, None, None, None], (slot_count, 1, row_cells, col_cells)
    )
    fluid_cells = to_block(fluid_tiles, x_bricks, y_bricks, z_cells, BR)[0]
    weight = fields[3]
    rim_stack = padded_2(jnp.stack([weight, fields[0], fields[1]]), (("gx", 2), ("yz", 1)), 1)
    rim_weight = rim_stack[0]
    face_z = jnp.sqrt(rim_weight[:-1, 1:-1] * rim_weight[1:, 1:-1])
    face_x = jnp.sqrt(rim_weight[1:-1, :-1] * rim_weight[1:-1, 1:])
    y_index = jnp.arange(weight.shape[2], dtype=jnp.int32)
    face_y = jnp.where(
        y_index < weight.shape[2] - 1, jnp.sqrt(weight * jnp.roll(weight, -1, 2)), 0.0
    )
    flux_z = face_z * (rim_stack[1][:-1, 1:-1] + rim_stack[1][1:, 1:-1]) * 0.5
    flux_x = face_x * (rim_stack[2][1:-1, :-1] + rim_stack[2][1:-1, 1:]) * 0.5
    flux_y = face_y * (fields[2] + jnp.roll(fields[2], -1, 2)) * 0.5
    source_term = (
        flux_z[:-1] - flux_z[1:] + flux_x[:, :-1] - flux_x[:, 1:] + jnp.roll(flux_y, 1, 2) - flux_y
    )
    diagonal = shift_rate * weight + (1.0 - fluid_cells) + face_z[:-1] + face_z[1:]
    diagonal = diagonal + face_x[:, :-1] + face_x[:, 1:] + face_y + jnp.roll(face_y, 1, 2)
    coefs = (face_z, face_x, face_y, diagonal)
    table_y = cosine_table(NY, NY, NY)
    table_x = cosine_table(NX, NX, NX)
    solution = jnp.zeros_like(source_term)
    residual = source_term
    update = precondition(residual, fluid_cells, table_y, table_x)
    image_of = operate(update, coefs)
    energy_now, curvature = paired(residual, update, image_of)
    step_size = energy_now / curvature
    direction = update
    along_dir = image_of
    for step_index in range(ITERS):
        solution = solution + step_size * direction
        residual = residual - step_size * along_dir
        if step_index + 1 < ITERS:
            update = precondition(residual, fluid_cells, table_y, table_x)
            image_of = operate(update, coefs)
            energy_next, curvature = paired(residual, update, image_of)
            beta_ratio = energy_next / energy_now
            step_size = energy_next / (curvature - beta_ratio * energy_next / step_size)
            direction = update + beta_ratio * direction
            along_dir = image_of + beta_ratio * along_dir
            energy_now = energy_next
    return (solution, residual)


def solution(mesh):
    return jax.shard_map(
        on_device,
        mesh=mesh,
        in_specs=(
            P("gx", "yz", None, None, None),
            P("gx", "yz", None, None),
            P("gx", "yz"),
            P("gx", "yz"),
        ),
        out_specs=(P("yz", "gx", None), P("yz", "gx", None)),
        check_vma=False,
    )
```

profile of v0, /device:TPU:0, one launch (start us, length us, event | category | flops | bytes accessed | tf_op | source)
XLA Modules:
  0.0 691.0 jit_solution(5577012599405391991)
XLA Ops:
  5.5 5.2 all-to-all-start.1
  16.7 4.3 all-to-all-start.2
  24.2 4.9 broadcast_select_fusion
  29.0 13.0 %all-to-all-done.2 = f32[8,24,16,128]{3,2,1,0:T(8,128)} async-done(((f32[8,24,16,128]{3,2,1,0:T(8,128)}), f32[8,24,16,128]{3,2,1,0:T(8,128)}, u32[]{:S(2)}, u32[]{:S(2)}) %all-to-all-start.2) | async-done | bytes 1572896 | tf_op jit(solution)/shard_map/all_to_all | solution.py:120
  42.1 4.6 all-to-all-start
  51.2 50.2 %all-to-all-done = f32[8,24,3,16,128]{4,3,2,1,0:T(8,128)} async-done(((f32[8,24,3,16,128]{4,3,2,1,0:T(8,128)}), f32[8,24,3,16,128]{4,3,2,1,0:T(8,128)}, u32[]{:S(2)}, u32[]{:S(2)}) %all-to-all-start) | async-done | bytes 4718624 | tf_op jit(solution)/shard_map/all_to_all | solution.py:119
  129.1 4.2 collective-permute-done.1
  133.7 4.9 copy.71
  157.8 4.0 slice_bitcast_fusion.1
  161.8 5.0 fusion.10
  169.0 20.2 %fusion.28 = f32[1,256,1024]{2,1,0:T(8,128)} fusion(s32[1024]{0:T(1024)S(1)} %multiply_add_fusion.1, f32[1024]{0:T(1024)S(1)} %get-tuple-element.40, f32[1,256,1024]{2,1,0:T(8,128)S(1)} %fusion.70), kind=kOutput, calls=%fused_computation.37 | convolution fusion | flops 3236954112 | bytes 2105344 | tf_op jit(solution)/shard_map/zxy,ky->zxk/dot_general | solution.py:71
  192.8 3.9 all-to-all-start.3
  196.7 15.9 %all-to-all-done.3 = f32[1,256,1024]{1,0,2:T(1,128)S(1)} async-done(((f32[1,256,1024]{1,0,2:T(1,128)}), f32[1,256,1024]{1,0,2:T(1,128)S(1)}, u32[]{:S(2)}, u32[]{:S(2)}) %all-to-all-start.3) | async-done | bytes 1048608 | tf_op jit(solution)/shard_map/all_to_all | solution.py:72
  215.2 23.1 %fusion.31 = f32[1,1024,256]{1,2,0:T(8,128)S(1)} fusion(f32[1024,256]{1,0:T(8,128)S(1)} %bitcast.140, s32[1024]{0:T(1024)S(1)} %multiply_add_fusion.1, f32[1024]{0:T(1024)S(1)} %get-tuple-element.40), kind=kOutput, calls=%fused_computation.38 | convolution fusion | flops 3236954112 | bytes 2105344 | tf_op jit(solution)/shard_map/kx,zxy->zky/dot_general | solution.py:80
  238.3 20.3 %fusion.34 = f32[1,1024,256]{1,2,0:T(8,128)} fusion(s32[1024]{0:T(1024)S(1)} %multiply_add_fusion.1, f32[1024]{0:T(1024)S(1)} %get-tuple-element.40, f32[1,1024,256]{1,2,0:T(8,128)S(1)} %fusion.31, f32[256]{0:T(256)S(1)} %multiply_subtract_fusion.4, f32[1024]{0:T(1024)S(1)} %get-tuple-element.39), kind=kOutput, calls=%fused_computation.39 | convolution fusion | flops 3237740544 | bytes 2110464 | tf_op jit(solution)/shard_map/kx,zky->zxy/dot_general | solution.py:81
  261.0 20.1 %all_to_all.76 = f32[1,1024,256]{2,0,1:T(1,128)S(1)} all-to-all(f32[1,1024,256]{2,0,1:T(1,128)S(1)} %copy.79), channel_id=1, replica_groups=mesh['gx'=4,'yz'=8] {'gx'}, dimensions={1} | all-to-all | bytes 2097152 | tf_op jit(solution)/shard_map/all_to_all | solution.py:82
  282.7 20.8 %fusion.46 = f32[256,1024]{1,0:T(8,128)S(1)} fusion(f32[256,1024]{0,1:T(8,128)} %bitcast.139, s32[1024]{0:T(1024)S(1)} %multiply_add_fusion.1, f32[1024]{0:T(1024)S(1)} %get-tuple-element.40, f32[32,8,8,128]{3,2,1,0:T(8,128)S(1)} %bitcast.136), kind=kOutput, calls=%fused_computation.43 | convolution fusion | flops 3237216256 | bytes 3153920 | tf_op jit(solution)/shard_map/zxk,ky->zxy/dot_general | solution.py:83
  306.9 4.2 collective-permute-done.5
  313.3 62.8 %collective-permute-start.6 = (f32[1,258,1024]{2,0,1:T(1,128)}, f32[1,258,1024]{2,0,1:T(1,128)}, u32[]{:S(2)}, u32[]{:S(2)}) collective-permute-start(f32[1,258,1024]{2,0,1:T(1,128)} %copy.81), channel_id=1, source_target_pairs={{0,1},{1,2},{2,3},{3,4},{4,5},{5,6},{6,7},{8,9},{9,10},{10,11},{11... | collective-permute-start | bytes 3170312 | tf_op jit(solution)/shard_map/ppermute | solution.py:24
  383.7 13.4 %collective-permute-done.7 = f32[1,258,1024]{2,0,1:T(1,128)} collective-permute-done((f32[1,258,1024]{2,0,1:T(1,128)}, f32[1,258,1024]{2,0,1:T(1,128)}, u32[]{:S(2)}, u32[]{:S(2)}) %collective-permute-start.7) | collective-permute-done | bytes 1056800 | tf_op jit(solution)/shard_map/ppermute | solution.py:27
  399.1 3.9 multiply_reduce_fusion.2
  403.0 54.1 %all-reduce.1 = (f32[]{:T(128)}, f32[]{:T(128)}) all-reduce(f32[]{:T(128)} %get-tuple-element.5, f32[]{:T(128)} %get-tuple-element.4), channel_id=1, replica_groups=mesh['gx'=4,'yz'=8] {'gx','yz'}, use_global_device_ids=true, to_apply=%region_6.7 | all-reduce | flops 2 | bytes 16 | tf_op jit(solution)/shard_map/psum | solution.py:88
  458.5 20.9 %fusion.37 = f32[1,256,1024]{2,1,0:T(8,128)S(1)} fusion(s32[1024]{0:T(1024)S(1)} %multiply_add_fusion.1, f32[1024]{0:T(1024)S(1)} %get-tuple-element.40, f32[1,256,1024]{2,1,0:T(8,128)} %copy-done.14, f32[1,256,1024]{2,1,0:T(8,128)} %get-tuple-element.11, f32[]{:T(128)S(6)} %div.47), kind=kOutput, calls=%fused_computation.40 | convolution fusion | flops 3237478400 | bytes 3153924 | tf_op jit(solution)/shard_map/zxy,ky->zxk/dot_general | solution.py:71
  480.2 28.5 %all_to_all.77 = f32[1,256,1024]{1,0,2:T(1,128)S(1)} all-to-all(f32[1,256,1024]{1,0,2:T(1,128)S(1)} %copy.85), channel_id=1, replica_groups=mesh['gx'=4,'yz'=8] {'gx'}, dimensions={2} | all-to-all | bytes 2097152 | tf_op jit(solution)/shard_map/all_to_all | solution.py:72
  509.1 22.9 %fusion.40 = f32[1,1024,256]{1,2,0:T(8,128)S(1)} fusion(f32[1024,256]{1,0:T(8,128)S(1)} %bitcast.141, s32[1024]{0:T(1024)S(1)} %multiply_add_fusion.1, f32[1024]{0:T(1024)S(1)} %get-tuple-element.40), kind=kOutput, calls=%fused_computation.41 | convolution fusion | flops 3236954112 | bytes 2105344 | tf_op jit(solution)/shard_map/kx,zxy->zky/dot_general | solution.py:80
  531.9 19.5 %fusion.43 = f32[1,1024,256]{1,2,0:T(8,128)S(1)} fusion(s32[1024]{0:T(1024)S(1)} %multiply_add_fusion.1, f32[1024]{0:T(1024)S(1)} %get-tuple-element.40, f32[1,1024,256]{1,2,0:T(8,128)S(1)} %fusion.40, f32[256]{0:T(256)S(1)} %multiply_subtract_fusion.4, f32[1024]{0:T(1024)S(1)} %get-tuple-element.39), kind=kOutput, calls=%fused_computation.42 | convolution fusion | flops 3237740544 | bytes 2110464 | tf_op jit(solution)/shard_map/kx,zky->zxy/dot_general | solution.py:81
  552.3 27.8 %all_to_all.78 = f32[1,1024,256]{2,0,1:T(1,128)S(1)} all-to-all(f32[1,1024,256]{2,0,1:T(1,128)S(1)} %copy.87), channel_id=1, replica_groups=mesh['gx'=4,'yz'=8] {'gx'}, dimensions={1} | all-to-all | bytes 2097152 | tf_op jit(solution)/shard_map/all_to_all | solution.py:82
  580.4 19.2 %fusion.49 = f32[256,1024]{1,0:T(8,128)S(1)} fusion(f32[256,1024]{0,1:T(8,128)S(1)} %bitcast.138, s32[1024]{0:T(1024)S(1)} %multiply_add_fusion.1, f32[1024]{0:T(1024)S(1)} %get-tuple-element.40, f32[32,8,8,128]{3,2,1,0:T(8,128)S(1)} %bitcast.137), kind=kOutput, calls=%fused_computation.44 | convolution fusion | flops 3237216256 | bytes 3153920 | tf_op jit(solution)/shard_map/zxk,ky->zxy/dot_general | solution.py:83
  603.2 4.2 collective-permute-done.9
  612.9 4.5 collective-permute-done.11
  618.2 4.0 multiply_reduce_fusion
  622.2 57.7 %all-reduce = (f32[]{:T(128)}, f32[]{:T(128)}) all-reduce(f32[]{:T(128)} %get-tuple-element.3, f32[]{:T(128)} %get-tuple-element.2), channel_id=1, replica_groups=mesh['gx'=4,'yz'=8] {'gx','yz'}, use_global_device_ids=true, to_apply=%region_10.11 | all-reduce | flops 2 | bytes 16 | tf_op jit(solution)/shard_map/psum | solution.py:88
  (160 shorter events, 110.9 us)
Async XLA Ops:
  0.6 20.4 %copy-start = (f32[1,128,3,16,128]{4,3,2,1,0:T(8,128)S(1)}, f32[1,128,3,16,128]{4,3,2,1,0:T(8,128)}, u32[]{:S(2)}) copy-start(f32[1,128,3,16,128]{4,3,2,1,0:T(8,128)} %param.4) | copy-start | bytes 9437188
  5.5 11.2 %all-to-all-start.1 = ((s32[8,1,24]{2,1,0:T(1,128)}), s32[8,1,24]{2,1,0:T(1,128)S(1)}, u32[]{:S(2)}, u32[]{:S(2)}) async-start(s32[8,1,24]{2,1,0:T(1,128)} %bitcast.8), calls=%async_computation.1 | async-start | bytes 8192 | tf_op jit(solution)/shard_map/all_to_all | solution.py:118
  16.7 25.3 %all-to-all-start.2 = ((f32[8,24,16,128]{3,2,1,0:T(8,128)}), f32[8,24,16,128]{3,2,1,0:T(8,128)}, u32[]{:S(2)}, u32[]{:S(2)}) async-start(f32[8,24,16,128]{3,2,1,0:T(8,128)} %broadcast_select_fusion.1), calls=%async_computation.2 | async-start | bytes 3145728 | tf_op jit(solution)/shard_map/all_to_all | solution.py:120
  29.0 17.6 %copy-start.24 = (s32[1,128]{1,0:T(1,128)S(1)}, s32[1,128]{1,0:T(1,128)}, u32[]{:S(2)}) copy-start(s32[1,128]{1,0:T(1,128)} %param.7) | copy-start | bytes 1540
  42.1 59.3 %all-to-all-start = ((f32[8,24,3,16,128]{4,3,2,1,0:T(8,128)}), f32[8,24,3,16,128]{4,3,2,1,0:T(8,128)}, u32[]{:S(2)}, u32[]{:S(2)}) async-start(f32[8,24,3,16,128]{4,3,2,1,0:T(8,128)} %broadcast_select_fusion), calls=%async_computation | async-start | bytes 9437184 | tf_op jit(solution)/shard_map/all_to_all | solution.py:119
  124.2 14.4 %copy-start.12 = (f32[3,1,256,1024]{3,2,1,0:T(8,128)}, f32[3,1,256,1024]{3,2,1,0:T(8,128)S(1)}, u32[]{:S(2)}) copy-start(f32[3,1,256,1024]{3,2,1,0:T(8,128)S(1)} %constant_dynamic-update-slice_fusion) | copy-start | bytes 9437188
  124.2 4.9 collective-permute-start
  127.7 5.6 collective-permute-start.1
  138.6 11.3 %collective-permute-start.2 = (f32[3,1,258,1024]{3,1,2,0:T(1,128)}, f32[3,1,258,1024]{3,1,2,0:T(1,128)}, u32[]{:S(2)}, u32[]{:S(2)}) collective-permute-start(f32[3,1,258,1024]{3,1,2,0:T(1,128)} %copy.71), channel_id=1, source_target_pairs={{0,1},{1,2},{2,3},{3,4},{4,5},{5,6},{6,7},{8,9},{9,10},{10,11},{11... | collective-permute-start | bytes 9510920 | tf_op jit(solution)/shard_map/ppermute | solution.py:24
  141.6 11.3 %collective-permute-start.3 = (f32[3,1,258,1024]{3,1,2,0:T(1,128)}, f32[3,1,258,1024]{3,1,2,0:T(1,128)}, u32[]{:S(2)}, u32[]{:S(2)}) collective-permute-start(f32[3,1,258,1024]{3,1,2,0:T(1,128)} %copy.71), channel_id=1, source_target_pairs={{1,0},{2,1},{3,2},{4,3},{5,4},{6,5},{7,6},{9,8},{10,9},{11,10},{12... | collective-permute-start | bytes 9510920 | tf_op jit(solution)/shard_map/ppermute | solution.py:27
  144.6 254.5 %copy-start.6 = (f32[1,256,1024]{2,1,0:T(8,128)}, f32[1,256,1024]{2,1,0:T(8,128)S(1)}, u32[]{:S(2)}) copy-start(f32[1,256,1024]{2,1,0:T(8,128)S(1)} %squeeze.34) | copy-start | bytes 3145732
  149.8 249.2 %copy-start.4 = (f32[1,256,1024]{2,1,0:T(8,128)}, f32[1,256,1024]{2,1,0:T(8,128)S(1)}, u32[]{:S(2)}) copy-start(f32[1,256,1024]{2,1,0:T(8,128)S(1)} %get-tuple-element.17) | copy-start | bytes 3145732
  168.9 20.3 %copy-start.14 = (f32[1,256,1024]{2,1,0:T(8,128)}, f32[1,256,1024]{2,1,0:T(8,128)S(1)}, u32[]{:S(2)}) copy-start(f32[1,256,1024]{2,1,0:T(8,128)S(1)} %fusion.70) | copy-start | bytes 3145732
  192.8 19.8 %all-to-all-start.3 = ((f32[1,256,1024]{1,0,2:T(1,128)}), f32[1,256,1024]{1,0,2:T(1,128)S(1)}, u32[]{:S(2)}, u32[]{:S(2)}) async-start(f32[1,256,1024]{1,0,2:T(1,128)} %copy.77), calls=%async_computation.3 | async-start | bytes 2097152 | tf_op jit(solution)/shard_map/all_to_all | solution.py:72
  282.6 20.8 %copy-start.22 = (f32[16,16,8,128]{3,2,1,0:T(8,128)}, f32[16,16,8,128]{3,2,1,0:T(8,128)S(1)}, u32[]{:S(2)}) copy-start(f32[16,16,8,128]{3,2,1,0:T(8,128)S(1)} %transpose.39) | copy-start | bytes 3145732
  303.5 95.6 %copy-start.2 = (f32[256,1024]{1,0:T(8,128)}, f32[256,1024]{1,0:T(8,128)S(1)}, u32[]{:S(2)}) copy-start(f32[256,1024]{1,0:T(8,128)S(1)} %fusion.46) | copy-start | bytes 3145732
  303.5 3.4 collective-permute-start.4
  305.6 5.5 collective-permute-start.5
  313.3 68.2 %collective-permute-start.6 = (f32[1,258,1024]{2,0,1:T(1,128)}, f32[1,258,1024]{2,0,1:T(1,128)}, u32[]{:S(2)}, u32[]{:S(2)}) collective-permute-start(f32[1,258,1024]{2,0,1:T(1,128)} %copy.81), channel_id=1, source_target_pairs={{0,1},{1,2},{2,3},{3,4},{4,5},{5,6},{6,7},{8,9},{9,10},{10,11},{11... | collective-permute-start | bytes 3170312 | tf_op jit(solution)/shard_map/ppermute | solution.py:24
  376.1 21.0 %collective-permute-start.7 = (f32[1,258,1024]{2,0,1:T(1,128)}, f32[1,258,1024]{2,0,1:T(1,128)}, u32[]{:S(2)}, u32[]{:S(2)}) collective-permute-start(f32[1,258,1024]{2,0,1:T(1,128)} %copy.81), channel_id=1, source_target_pairs={{1,0},{2,1},{3,2},{4,3},{5,4},{6,5},{7,6},{9,8},{10,9},{11,10},{12... | collective-permute-start | bytes 3170312 | tf_op jit(solution)/shard_map/ppermute | solution.py:27
  381.1 18.0 %copy-start.8 = (f32[1,257,1024]{2,1,0:T(8,128)S(1)}, f32[1,257,1024]{2,1,0:T(8,128)}, u32[]{:S(2)}) copy-start(f32[1,257,1024]{2,1,0:T(8,128)} %get-tuple-element.15) | copy-start | bytes 3158020
  381.1 18.0 %copy-start.10 = (f32[2,256,1024]{2,1,0:T(8,128)S(1)}, f32[2,256,1024]{2,1,0:T(8,128)}, u32[]{:S(2)}) copy-start(f32[2,256,1024]{2,1,0:T(8,128)} %get-tuple-element.13) | copy-start | bytes 6291460
  381.1 18.0 %copy-start.15 = (f32[1,256,1024]{2,1,0:T(8,128)S(1)}, f32[1,256,1024]{2,1,0:T(8,128)}, u32[]{:S(2)}) copy-start(f32[1,256,1024]{2,1,0:T(8,128)} %copy-done.14) | copy-start | bytes 3145732
  381.1 18.0 %copy-start.18 = (f32[1,256,1024]{2,1,0:T(8,128)S(1)}, f32[1,256,1024]{2,1,0:T(8,128)}, u32[]{:S(2)}) copy-start(f32[1,256,1024]{2,1,0:T(8,128)} %sub.88) | copy-start | bytes 3145732
  551.5 29.0 %copy-start.23 = (f32[16,16,8,128]{3,2,1,0:T(8,128)S(1)}, f32[16,16,8,128]{3,2,1,0:T(8,128)}, u32[]{:S(2)}) copy-start(f32[16,16,8,128]{3,2,1,0:T(8,128)} %copy-done.22) | copy-start | bytes 3145732
  599.7 18.4 %copy-start.3 = (f32[256,1024]{1,0:T(8,128)}, f32[256,1024]{1,0:T(8,128)S(1)}, u32[]{:S(2)}) copy-start(f32[256,1024]{1,0:T(8,128)S(1)} %fusion.49) | copy-start | bytes 3145732
  599.7 3.4 collective-permute-start.8
  601.8 5.5 collective-permute-start.9
  608.6 3.6 collective-permute-start.10
  610.0 7.4 %collective-permute-start.11 = (f32[1,258,1024]{2,0,1:T(1,128)S(1)}, f32[1,258,1024]{2,0,1:T(1,128)S(1)}, u32[]{:S(2)}, u32[]{:S(2)}) collective-permute-start(f32[1,258,1024]{2,0,1:T(1,128)S(1)} %copy.89), channel_id=1, source_target_pairs={{1,0},{2,1},{3,2},{4,3},{5,4},{6,5},{7,6},{9,8},{10,9},{11,10},{12... | collective-permute-start | bytes 3170312 | tf_op jit(solution)/shard_map/ppermute | solution.py:27
  611.5 6.6 copy-start.19
  618.2 72.4 %copy-start.1 = (f32[1,128,3,16,128]{4,3,2,1,0:T(8,128)S(1)}, f32[1,128,3,16,128]{4,3,2,1,0:T(8,128)}, u32[]{:S(2)}) copy-start(f32[1,128,3,16,128]{4,3,2,1,0:T(8,128)} %param.4) | copy-start | bytes 9437188
  (9 other events, 48.0 us)
where the time goes:
time: 700 us; the launch traced here: 691 us
  blocking collectives  188 us (27%)
  matrix products  167 us (24%)
  waiting for transfers between devices  110 us (16%)
  starting transfers between devices  101 us (14%)
  local copies, waits for them, and re-layouts  78.6 us (11%)
  other arithmetic  38.5 us (6%)
  between operations  7.88 us (1%)
    psum x2, blocking collectives, paired(): lax.psum((jnp.sum(residual * update), jnp.sum(image_of * update)), ('gx',...  112 us
    ppermute x6, starting transfers between devices, padded_2(): lax.ppermute(lax.slice_in_dim(block, block.shape[dim] - width, None, axis...  74.9 us
    all_to_all x1, waiting for transfers between devices, on_device(): lax.all_to_all(send_accel, 'yz', split_axis=0, concat_axis=0, tiled=True)  50.2 us
    all_to_all x2, blocking collectives, precondition(): lax.all_to_all(spatial, 'gx', split_axis=1, concat_axis=2, tiled=True)  47.9 us
    dot_general x2, matrix products, precondition(): jnp.einsum('kx,zxy->zky', table_x, pencil, precision=highest) / denom[None]  46 us
    dot_general x2, matrix products, precondition(): spectrum = jnp.einsum('zxy,ky->zxk', residual, table_y, precision=highest)  41.2 us
    dot_general x2, matrix products, precondition(): spatial_out = jnp.einsum('zxk,ky->zxy', mixed, table_y, precision=highest)  40 us
    dot_general x2, matrix products, precondition(): spatial = jnp.einsum('kx,zky->zxy', table_x, modes, precision=highest)  39.8 us
  transfers between devices with their start and end apart: 16, of which 10 were waited for; matrix products, arithmetic and copies ran while one was open for 5% of the time, Pallas kernels for 0%

commit v1 on v0

v1 whole, which is shorter than its diff:
```python
import functools

import jax
import jax.numpy as jnp
import ml_dtypes
import numpy as np
from jax import lax
from jax.experimental import pallas as pl
from jax.experimental.pallas import tpu as pltpu
from jax.sharding import PartitionSpec as P

NX = 1024
NY = 1024
BR = 16
B = 128
ITERS = 2

shift_rate = 0.05
spectral_gain = 1.0
spectral_floor = 2.0

MESH = pl.DeviceIdType.MESH
PAD = 8
CHUNK = 16
TILE = 256


def cosine_table(length):
    rows = np.arange(length, dtype=np.int64)[:, None]
    cols = np.arange(length, dtype=np.int64)[None, :]
    phases = (rows * (2 * cols + 1)) % (4 * length)
    scale = np.sqrt(np.where(rows == 0, 1.0, 2.0) / length)
    return scale * np.cos(phases * (np.pi / (2.0 * length)))


def eigen_values(length):
    return 2.0 - 2.0 * np.cos(np.arange(length) * (np.pi / length))


def high_low(table):
    high = table.astype(np.float32).astype(ml_dtypes.bfloat16)
    low = (table - high.astype(np.float64)).astype(np.float32).astype(ml_dtypes.bfloat16)
    return np.stack([high, low])


def solver_tables(slabs, rows):
    table_y = cosine_table(NY)
    table_x = cosine_table(rows)
    inverse = 1.0 / (
        spectral_gain * (eigen_values(rows)[:, None] + eigen_values(NY)[None, :]) + spectral_floor
    )
    first, last = table_x[:, :1], table_x[:, -1:]
    same = np.sum(first * first * inverse, axis=0)
    cross = np.sum(first * last * inverse, axis=0)
    faces = slabs - 1
    couple = np.zeros((slabs, 2, 2 * slabs, NY))
    if faces:
        matrix = np.zeros((NY, faces, faces))
        for i in range(faces):
            matrix[:, i, i] = 1.0 / spectral_gain + 2.0 * same
            if i:
                matrix[:, i, i - 1] = matrix[:, i - 1, i] = -cross
        solved = np.linalg.inv(matrix)
        for slab in range(slabs):
            for side, face, sign in ((0, slab - 1, 1.0), (1, slab, -1.0)):
                if 0 <= face < faces:
                    for other in range(faces):
                        couple[slab, side, 2 * other + 1] += sign * solved[:, face, other]
                        couple[slab, side, 2 * other + 2] -= sign * solved[:, face, other]
    ends = np.concatenate([np.repeat(first, B, 1), np.repeat(last, B, 1)], axis=1)
    return (
        high_low(table_y.T),
        high_low(table_y),
        high_low(table_x),
        high_low(table_x.T),
        inverse.astype(np.float32),
        ends.astype(np.float32),
        couple.astype(np.float32),
    )


def exchange_kernel(owners, per_owner, src_ref, accel_ref, weight_ref, out_ref, send, send_sem, recv_sem):
    me = lax.axis_index("yz")
    barrier = pltpu.get_barrier_semaphore()
    for k in range(1, owners):
        pl.semaphore_signal(
            barrier, inc=1, device_id={"yz": lax.rem(me + k, owners)}, device_id_type=MESH
        )
    pl.semaphore_wait(barrier, owners - 1)

    def pack(k, owner):
        def one(p, carry):
            slot = src_ref[owner * per_owner + p]
            send[k, p, 0] = weight_ref[slot]
            send[k, p, 1] = accel_ref[slot, 0]
            send[k, p, 2] = accel_ref[slot, 1]
            send[k, p, 3] = accel_ref[slot, 2]
            return carry

        lax.fori_loop(0, per_owner, one, 0)

    copies = []
    for k in range(1, owners):
        owner = lax.rem(me + k, owners)
        pack(k, owner)
        copy = pltpu.make_async_remote_copy(
            src_ref=send.at[k],
            dst_ref=out_ref.at[me],
            send_sem=send_sem.at[k],
            recv_sem=recv_sem.at[k],
            device_id={"yz": owner},
            device_id_type=MESH,
        )
        copy.start()
        copies.append(copy)
    pack(0, me)
    own = pltpu.make_async_copy(send.at[0], out_ref.at[me], send_sem.at[0])
    own.start()
    own.wait()
    for copy in copies:
        copy.wait()


def exchange(source, accel, weight, owners, per_owner):
    slots, _, row_cells, col_cells = accel.shape
    shape = (owners, per_owner, 4, row_cells, col_cells)
    return pl.pallas_call(
        functools.partial(exchange_kernel, owners, per_owner),
        out_shape=jax.ShapeDtypeStruct(shape, jnp.float32),
        in_specs=[
            pl.BlockSpec(memory_space=pltpu.SMEM),
            pl.BlockSpec(memory_space=pltpu.VMEM),
            pl.BlockSpec(memory_space=pltpu.VMEM),
        ],
        out_specs=pl.BlockSpec(memory_space=pl.ANY),
        scratch_shapes=[
            pltpu.VMEM(shape, jnp.float32),
            pltpu.SemaphoreType.DMA((owners,)),
            pltpu.SemaphoreType.DMA((owners,)),
        ],
        compiler_params=pltpu.CompilerParams(
            collective_id=0, has_side_effects=True, vmem_limit_bytes=40 * 2**20
        ),
        name="brick_exchange",
    )(source, accel, weight)


def split(value):
    high = value.astype(jnp.bfloat16)
    return high, (value - high.astype(jnp.float32)).astype(jnp.bfloat16)


def dot32(left, right):
    return jnp.dot(left, right, preferred_element_type=jnp.float32)


def solver_kernel(
    slabs, owners, rows, y_bricks,
    anchor_ref, fluid_ref, bricks_ref, fwd_hbm, inv_hbm, table_x, table_xt, inverse_ref, ends_ref, couple_ref,
    solution_ref, residual_ref,
    fwd, inv, root, accel_x, accel_y, accel_z, fluid, diagonal, near_root, near_accel, near_t, t_pad,
    res_hl, spec, x_hl, update, image, edge, gathered, part, total_yz, total_gx,
    table_sem, near_sem, row_sem, t_sem, t_row_sem, edge_sem, yz_sem, gx_sem,
):
    g = lax.axis_index("gx")
    z = lax.axis_index("yz")
    barrier = pltpu.get_barrier_semaphore()
    for k in range(1, owners):
        pl.semaphore_signal(barrier, inc=1, device_id={"yz": lax.rem(z + k, owners)}, device_id_type=MESH)
    for k in range(1, slabs):
        pl.semaphore_signal(barrier, inc=1, device_id={"gx": lax.rem(g + k, slabs)}, device_id_type=MESH)

    table_copies = [
        pltpu.make_async_copy(fwd_hbm, fwd, table_sem.at[0]),
        pltpu.make_async_copy(inv_hbm, inv, table_sem.at[1]),
    ]
    for copy in table_copies:
        copy.start()

    has_low, has_high = z > 0, z < owners - 1
    has_prev, has_next = g > 0, g < slabs - 1

    def remote(src, dst, sems, device):
        return pltpu.make_async_remote_copy(
            src_ref=src, dst_ref=dst, send_sem=sems.at[0], recv_sem=sems.at[1],
            device_id=device, device_id_type=MESH,
        )

    def plane_copies(src, near, sems):
        up = remote(src, near.at[0], sems.at[0], {"yz": jnp.minimum(z + 1, owners - 1)})
        down = remote(src, near.at[1], sems.at[1], {"yz": jnp.maximum(z - 1, 0)})
        return up, down

    def row_copies(buf, sems):
        after = remote(
            buf.at[pl.ds(rows, PAD)], buf.at[pl.ds(0, PAD)], sems.at[0],
            {"gx": jnp.minimum(g + 1, slabs - 1)},
        )
        before = remote(
            buf.at[pl.ds(PAD, PAD)], buf.at[pl.ds(PAD + rows, PAD)], sems.at[1],
            {"gx": jnp.maximum(g - 1, 0)},
        )
        return after, before

    def start_pair(pair, to_first, to_second):
        @pl.when(to_first)
        def _():
            pair[0].start()

        @pl.when(to_second)
        def _():
            pair[1].start()

    def wait_pair(pair, has_before, has_after):
        @pl.when(has_after)
        def _():
            pair[0].wait_send()
            pair[1].wait_recv()

        @pl.when(has_before)
        def _():
            pair[1].wait_send()
            pair[0].wait_recv()

    def clear_rows(buf):
        @pl.when(jnp.logical_not(has_prev))
        def _():
            buf[pl.ds(0, PAD)] = jnp.zeros((PAD, NY), jnp.float32)

        @pl.when(jnp.logical_not(has_next))
        def _():
            buf[pl.ds(PAD + rows, PAD)] = jnp.zeros((PAD, NY), jnp.float32)

    def clear_planes(near):
        @pl.when(jnp.logical_not(has_low))
        def _():
            near[0] = jnp.zeros((rows, NY), jnp.float32)

        @pl.when(jnp.logical_not(has_high))
        def _():
            near[1] = jnp.zeros((rows, NY), jnp.float32)

    def place(b, carry):
        slot = anchor_ref[b]
        keep = fluid_ref[b]
        r0 = pl.multiple_of((b // y_bricks) * BR, BR)
        c0 = pl.multiple_of((b % y_bricks) * B, B)
        at = (pl.ds(r0, BR), pl.ds(c0, B))
        at_pad = (pl.ds(pl.multiple_of(r0 + PAD, PAD), BR), pl.ds(c0, B))
        root[at_pad] = jnp.sqrt(bricks_ref[slot, 0] * keep)
        accel_z[at] = bricks_ref[slot, 1] * keep
        accel_x[at_pad] = bricks_ref[slot, 2] * keep
        accel_y[at] = bricks_ref[slot, 3] * keep
        fluid[at] = jnp.full((BR, B), keep, jnp.float32)
        return carry

    lax.fori_loop(0, rows // BR * y_bricks, place, 0)

    pl.semaphore_wait(barrier, owners + slabs - 2)
    root_rows = root.at[pl.ds(PAD, rows)]
    near_pairs = [
        plane_copies(root_rows, near_root, near_sem.at[0]),
        plane_copies(accel_z, near_accel, near_sem.at[1]),
    ]
    row_pairs = [row_copies(root, row_sem.at[0]), row_copies(accel_x, row_sem.at[1])]
    for pair in row_pairs:
        start_pair(pair, has_next, has_prev)
    for pair in near_pairs:
        start_pair(pair, has_high, has_low)
    for buf in (root, accel_x, t_pad.at[0], t_pad.at[1]):
        clear_rows(buf)
    for buf in (near_root, near_accel, near_t.at[0], near_t.at[1]):
        clear_planes(buf)
    for pair in row_pairs:
        wait_pair(pair, has_prev, has_next)
    for pair in near_pairs:
        wait_pair(pair, has_low, has_high)

    lane = lax.broadcasted_iota(jnp.int32, (CHUNK, NY), 1)

    def left(value):
        return jnp.where(lane == 0, 0.0, pltpu.roll(value, 1, 1))

    def right(value):
        return jnp.where(lane == NY - 1, 0.0, pltpu.roll(value, NY - 1, 1))

    def at_chunk(i):
        r0 = pl.multiple_of(i * CHUNK, CHUNK)
        return pl.ds(r0, CHUNK), pl.ds(r0, CHUNK + 2 * PAD)

    def shifts(wide):
        return (
            wide[PAD - 1 : PAD - 1 + CHUNK],
            wide[PAD : PAD + CHUNK],
            wide[PAD + 1 : PAD + 1 + CHUNK],
        )

    def store_residual(at, value):
        residual_ref[0, at, :] = value
        high, low = split(value)
        res_hl[0, at, :] = high
        res_hl[1, at, :] = low

    def prepare(i, carry):
        at, wide_at = at_chunk(i)
        s_wide = root[wide_at, :]
        s_up, s, s_down = shifts(s_wide)
        ax_wide = accel_x[wide_at, :]
        ax = ax_wide[PAD : PAD + CHUNK]
        px_up, _, px_down = shifts(s_wide * ax_wide)
        ay = accel_y[at, :]
        py = s * ay
        s_left, s_right = left(s), right(s)
        s_low, s_high = near_root[0, at, :], near_root[1, at, :]
        az = accel_z[at, :]
        total = px_up - px_down + ax * (s_up - s_down)
        total = total + left(py) - right(py) + ay * (s_left - s_right)
        total = total + s_low * near_accel[0, at, :] - s_high * near_accel[1, at, :] + az * (s_low - s_high)
        store_residual(at, 0.5 * s * total)
        ring = s_up + s_down + s_left + s_right + s_low + s_high
        diagonal[at, :] = s * (shift_rate * s + ring) + (1.0 - fluid[at, :])
        return carry

    chunks = rows // CHUNK
    lax.fori_loop(0, chunks, prepare, 0)
    for copy in table_copies:
        copy.wait()

    tiles = NY // TILE

    def three(left_hl, right_hl):
        lh, ll = left_hl
        rh, rl = right_hl
        return dot32(lh, rh) + dot32(lh, rl) + dot32(ll, rh)

    def tile_at(j):
        return pl.ds(pl.multiple_of(j * TILE, TILE), TILE)

    def precondition(it):
        def forward(j, carry):
            at = tile_at(j)
            lines = three((res_hl[0], res_hl[1]), (fwd[0, :, at], fwd[1, :, at]))
            modes = three((table_x[0], table_x[1]), split(lines)) * inverse_ref[:, at]
            spec[:, at] = modes
            edge[it, 0:1, at] = jnp.sum(modes * ends_ref[:, 0:1], axis=0, keepdims=True)
            edge[it, 1:2, at] = jnp.sum(modes * ends_ref[:, B : B + 1], axis=0, keepdims=True)
            return carry

        edge[it] = jnp.zeros((8, NY), jnp.float32)
        lax.fori_loop(0, tiles, forward, 0)
        copies = [
            remote(edge.at[it], gathered.at[it, g], edge_sem.at[it, k], {"gx": lax.rem(g + k, slabs)})
            for k in range(1, slabs)
        ]
        for copy in copies:
            copy.start()
        gathered[it, g] = edge[it]
        for copy in copies:
            copy.wait()
        sides = []
        for side in range(2):
            total = jnp.zeros((1, NY), jnp.float32)
            for j in range(slabs):
                for end in range(2):
                    n = 2 * j + end
                    total = total + couple_ref[g, side, n : n + 1, :] * gathered[it, j, end : end + 1, :]
            sides.append(total)
        edge_y = jnp.concatenate(sides, axis=0)
        part[0:2, :] = edge_y

        def back_x(j, carry):
            at = tile_at(j)
            fix = ends_ref[:, 0:1] * part[0:1, at] + ends_ref[:, B : B + 1] * part[1:2, at]
            modes = spec[:, at] + inverse_ref[:, at] * fix
            high, low = split(three((table_xt[0], table_xt[1]), split(modes)))
            x_hl[0, :, at] = high
            x_hl[1, :, at] = low
            return carry

        lax.fori_loop(0, tiles, back_x, 0)
        pairs = []
        for j in range(tiles):
            at = pl.ds(j * TILE, TILE)
            out = three((x_hl[0], x_hl[1]), (inv[0, :, at], inv[1, :, at])) * fluid[:, at]
            update[it, :, at] = out
            t_pad[it, pl.ds(PAD, rows), at] = out * root[pl.ds(PAD, rows), at]
            pair = plane_copies(
                t_pad.at[it, pl.ds(PAD, rows), at], near_t.at[it, :, :, at], t_sem.at[it, j]
            )
            start_pair(pair, has_high, has_low)
            pairs.append(pair)
        rim = row_copies(t_pad.at[it], t_row_sem.at[it])
        start_pair(rim, has_next, has_prev)
        wait_pair(rim, has_prev, has_next)
        for pair in pairs:
            wait_pair(pair, has_low, has_high)

    def operate(it):
        def one(i, carry):
            energy, curve = carry
            at, wide_at = at_chunk(i)
            t_up, t, t_down = shifts(t_pad[it, wide_at, :])
            _, s, _ = shifts(root[wide_at, :])
            near = t_up + t_down + left(t) + right(t) + near_t[it, 0, at, :] + near_t[it, 1, at, :]
            u = update[it, at, :]
            out = diagonal[at, :] * u - s * near
            image[it, at, :] = out
            return energy + u * residual_ref[0, at, :], curve + u * out

        zero = jnp.zeros((CHUNK, NY), jnp.float32)
        energy, curve = lax.fori_loop(0, chunks, one, (zero, zero))
        row = lax.broadcasted_iota(jnp.int32, (8, B), 0)
        block = jnp.where(row < 4, jnp.sum(energy), jnp.sum(curve))
        for buf, sems, axis, count, index in (
            (total_yz, yz_sem, "yz", owners, z),
            (total_gx, gx_sem, "gx", slabs, g),
        ):
            buf[it, index] = block
            copies = [
                remote(buf.at[it, index], buf.at[it, index], sems.at[it, k], {axis: lax.rem(index + k, count)})
                for k in range(1, count)
            ]
            for copy in copies:
                copy.start()
            for copy in copies:
                copy.wait()
            block = buf[it, 0]
            for k in range(1, count):
                block = block + buf[it, k]
        return block[0:1, 0:1], block[4:5, 0:1]

    precondition(0)
    energy_now, curvature = operate(0)
    step_now = energy_now / curvature

    def advance(i, carry):
        at, _ = at_chunk(i)
        store_residual(at, residual_ref[0, at, :] - step_now * image[0, at, :])
        return carry

    lax.fori_loop(0, chunks, advance, 0)
    precondition(1)
    energy_next, curvature = operate(1)
    beta = energy_next / energy_now
    step_next = energy_next / (curvature - beta * energy_next / step_now)

    def finish(i, carry):
        at, _ = at_chunk(i)
        first, second = update[0, at, :], update[1, at, :]
        solution_ref[0, at, :] = step_now * first + step_next * (second + beta * first)
        residual_ref[0, at, :] = residual_ref[0, at, :] - step_next * (
            image[1, at, :] + beta * image[0, at, :]
        )
        return carry

    lax.fori_loop(0, chunks, finish, 0)


def solve(anchor, fluid, bricks, slabs, owners, rows, y_bricks):
    tables = [jnp.asarray(t) for t in solver_tables(slabs, rows)]
    plane = (rows, NY)
    padded = (rows + 2 * PAD, NY)
    f32, bf16 = jnp.float32, jnp.bfloat16
    vmem = pl.BlockSpec(memory_space=pltpu.VMEM)
    smem = pl.BlockSpec(memory_space=pltpu.SMEM)
    hbm = pl.BlockSpec(memory_space=pl.ANY)
    dma = pltpu.SemaphoreType.DMA
    out = jax.ShapeDtypeStruct((1,) + plane, f32)
    return pl.pallas_call(
        functools.partial(solver_kernel, slabs, owners, rows, y_bricks),
        out_shape=(out, out),
        in_specs=[smem, smem, vmem, hbm, hbm] + [vmem] * 5,
        out_specs=(vmem, vmem),
        scratch_shapes=[
            pltpu.VMEM((2, NY, NY), bf16),
            pltpu.VMEM((2, NY, NY), bf16),
            pltpu.VMEM(padded, f32),
            pltpu.VMEM(padded, f32),
            pltpu.VMEM(plane, f32),
            pltpu.VMEM(plane, f32),
            pltpu.VMEM(plane, f32),
            pltpu.VMEM(plane, f32),
            pltpu.VMEM((2,) + plane, f32),
            pltpu.VMEM((2,) + plane, f32),
            pltpu.VMEM((ITERS, 2) + plane, f32),
            pltpu.VMEM((ITERS,) + padded, f32),
            pltpu.VMEM((2,) + plane, bf16),
            pltpu.VMEM(plane, f32),
            pltpu.VMEM((2,) + plane, bf16),
            pltpu.VMEM((ITERS,) + plane, f32),
            pltpu.VMEM((ITERS,) + plane, f32),
            pltpu.VMEM((ITERS, 8, NY), f32),
            pltpu.VMEM((ITERS, slabs, 8, NY), f32),
            pltpu.VMEM((8, NY), f32),
            pltpu.VMEM((ITERS, owners, 8, B), f32),
            pltpu.VMEM((ITERS, slabs, 8, B), f32),
            dma((2,)),
            dma((2, 2, 2)),
            dma((2, 2, 2)),
            dma((ITERS, NY // TILE, 2, 2)),
            dma((ITERS, 2, 2)),
            dma((ITERS, slabs, 2)),
            dma((ITERS, owners, 2)),
            dma((ITERS, slabs, 2)),
        ],
        compiler_params=pltpu.CompilerParams(
            collective_id=1, has_side_effects=True, vmem_limit_bytes=60 * 2**20
        ),
        name="pressure_solver",
    )(anchor, fluid, bricks, *tables)


def ranks_of(owners_of, owner_count):
    one_hot = (owners_of[..., None] == jnp.arange(owner_count, dtype=jnp.int32)).astype(jnp.int32)
    earlier = jnp.cumsum(one_hot, axis=-2) - one_hot
    return jnp.sum(earlier * one_hot, axis=-1)


def on_device(camera_accel, camera_weight, brick_slot, brick_solid):
    owner_count = lax.axis_size("yz")
    slabs = lax.axis_size("gx")
    slot_count = brick_slot.shape[1]
    per_owner = 3 * slot_count // (2 * owner_count)
    rows = NX // slabs
    y_bricks = NY // B
    me = lax.axis_index("yz")
    slots = jnp.arange(slot_count, dtype=jnp.int32)

    brick_ids = brick_slot[0]
    owners_of = brick_ids // slot_count
    target = owners_of * per_owner + ranks_of(owners_of, owner_count)
    positions = jnp.arange(owner_count * per_owner, dtype=jnp.int32)
    matches = target[None, :] == positions[:, None]
    source = jnp.sum(jnp.where(matches, slots[None, :], 0), axis=1)

    all_ids = lax.all_gather(brick_ids, "yz")
    mine = all_ids // slot_count == me
    earlier = jnp.cumsum(mine.astype(jnp.int32), axis=1) - mine.astype(jnp.int32)
    place_of = jnp.arange(owner_count, dtype=jnp.int32)[:, None] * per_owner + earlier
    wanted = me * slot_count + slots
    arrived = all_ids.reshape(-1)[None, :] == wanted[:, None]
    anchor = jnp.sum(jnp.where(arrived, place_of.reshape(-1)[None, :], 0), axis=1)

    bricks = exchange(source, camera_accel[0], camera_weight[0], owner_count, per_owner)
    bricks = bricks.reshape((owner_count * per_owner,) + bricks.shape[2:])
    fluid = (1 - brick_solid[0]).astype(jnp.float32)
    return solve(anchor, fluid, bricks, slabs, owner_count, rows, y_bricks)


def solution(mesh):
    return jax.shard_map(
        on_device,
        mesh=mesh,
        in_specs=(
            P("gx", "yz", None, None, None),
            P("gx", "yz", None, None),
            P("gx", "yz"),
            P("gx", "yz"),
        ),
        out_specs=(P("yz", "gx", None), P("yz", "gx", None)),
        check_vma=False,
    )
```

time: 700 us -> 243 us (0.35); the launches traced: 691 us -> 243 us
  Pallas kernels: 0 us -> 217 us
  blocking collectives: 188 us -> 10.3 us
  matrix products: 167 us -> 0 us
  waiting for transfers between devices: 110 us -> 0 us
  starting transfers between devices: 101 us -> 0 us
  local copies, waits for them, and re-layouts: 78.6 us -> 10.4 us
  other arithmetic: 38.5 us -> 4.13 us
  between operations: 7.88 us -> 0.69 us
    pallas_call x0 -> x2, Pallas kernels: none -> 217 us  [the longest x1 147 us: solve(): pl.pallas_call(functools.partial(solver_kernel, slabs, owners, rows, y_br...]
    dot_general x8 -> x0, matrix products: 167 us -> none  [the longest x2 46 us: precondition(): jnp.einsum('kx,zxy->zky', table_x, pencil, precision=highest) / denom[None]]
    psum x2 -> x0, blocking collectives: 112 us -> none  [paired(): lax.psum((jnp.sum(residual * update), jnp.sum(image_of * update)), ('gx',...]
    ppermute x12 -> x0, starting transfers between devices: 83.1 us -> none  [the longest x6 74.9 us: padded_2(): lax.ppermute(lax.slice_in_dim(block, block.shape[dim] - width, None, axis...]
    all_to_all x4 -> x0, waiting for transfers between devices: 79.1 us -> none  [the longest x1 50.2 us: on_device(): lax.all_to_all(send_accel, 'yz', split_axis=0, concat_axis=0, tiled=True)]
    all_to_all x3 -> x0, blocking collectives: 76.3 us -> none  [the longest x2 47.9 us: precondition(): lax.all_to_all(spatial, 'gx', split_axis=1, concat_axis=2, tiled=True)]
    ppermute x12 -> x0, waiting for transfers between devices: 30.7 us -> none  [the longest x6 30.5 us: padded_2(): lax.ppermute(lax.slice_in_dim(block, 0, width, axis=dim), axis, backward)]
    slice x25 -> x0, local copies, waits for them, and re-layouts: 23 us -> none  [the longest x3 6.7 us: on_device(): fields[1]]
  transfers between devices with their start and end apart: 16 -> 0, of which waited for: 10 -> 0; matrix products, arithmetic and copies ran while one was open for 5% -> 0% of each run, Pallas kernels for 0% -> 0%
where the time goes in v1:
time: 243 us
  Pallas kernels  217 us (89%)
  local copies, waits for them, and re-layouts  10.4 us (4%)
  blocking collectives  10.3 us (4%)
  other arithmetic  4.13 us (2%)
    pallas_call x1, Pallas kernels, solve(): pl.pallas_call(functools.partial(solver_kernel, slabs, owners, rows, y_br...  147 us
    pallas_call x1, Pallas kernels, exchange(): pl.pallas_call(functools.partial(exchange_kernel, owners, per_owner), out...  70.7 us
    unnamed x8, local copies, waits for them, and re-layouts  10.4 us
    all_gather x1, blocking collectives, on_device(): all_ids = lax.all_gather(brick_ids, 'yz')  10.3 us

profile of v1, /device:TPU:0, one launch (start us, length us, event | category | flops | bytes accessed | tf_op | source)
XLA Modules:
  0.0 242.8 jit_solution(3570126106546322730)
XLA Ops:
  0.6 0.7 and_select_fusion
  1.3 1.2 convert_bitcast_fusion.fluid_ref
  2.5 10.3 %all-gather = s32[8,1,128]{2,1,0:T(1,128)S(1)} all-gather(s32[1,1,128]{2,1,0:T(1,128)} %bitcast.30), channel_id=1, replica_groups=mesh['gx'=4,'yz'=8] {'yz'}, dimensions={0}, use_global_device_ids=true | all-gather | bytes 4608 | tf_op jit(solution)/shard_map/all_gather | solution.py:536
  12.8 0.3 reduce_window_sum.22
  13.1 0.1 add_bitcast_fusion
  13.1 0.7 select_reduce_fusion.anchor_ref
  13.9 0.1 fusion
  13.9 0.2 reduce_window_sum.23
  14.1 0.2 select_reduce_fusion.2
  14.3 0.7 fusion.5
  15.0 0.1 select_reduce_fusion.1.src_ref
  15.1 0.0 copy-start.1
  15.1 1.9 copy-done.1
  17.0 0.0 copy-start.2
  17.0 1.2 copy-done.2
  18.2 70.7 %brick_exchange.1 = f32[8,24,4,16,128]{4,3,2,1,0:T(8,128)S(1)} custom-call(s32[192]{0:T(256)S(1)} %select_reduce_fusion.1.src_ref, f32[128,3,16,128]{3,2,1,0:T(8,128)S(1)} %bitcast.25, f32[128,16,128]{2,1,0:T(8,128)S(1)} %bitcast.26), custom_call_target="tpu_custom_call" | custom-call | tf_op jit(solution)/shard_map/brick_exchange/pallas_call | solution.py:127
  88.9 0.0 copy-start
  89.0 2.7 %copy-done = f32[8,24,4,16,128]{4,3,2,1,0:T(8,128)} copy-done((f32[8,24,4,16,128]{4,3,2,1,0:T(8,128)}, f32[8,24,4,16,128]{4,3,2,1,0:T(8,128)S(1)}, u32[]{:S(2)}) %copy-start) | copy-done | bytes 6291480
  91.6 146.5 %pressure_solver.1 = (f32[1,256,1024]{2,1,0:T(8,128)}, f32[1,256,1024]{2,1,0:T(8,128)}) custom-call(s32[128]{0:T(128)} %select_reduce_fusion.anchor_ref, f32[128]{0:T(128)} %convert_bitcast_fusion.fluid_ref, f32[192,4,16,128]{3,2,1,0:T(8,128)} %bitcast.24, bf16[2,1024,1024]{2,1,0:T(8,128)(2,1)} %constant.56.clone.fwd_hbm, ...), custom_call_target="tpu_custom_call" | custom-call | tf_op jit(solution)/shard_map/pressure_solver/pallas_call | solution.py:469
  238.1 2.3 copy.16
  240.5 2.3 copy.17
  (3 shorter events, 0.0 us)
Async XLA Ops:
  15.1 1.9 copy-start.1
  17.0 1.2 copy-start.2
  88.9 2.7 %copy-start = (f32[8,24,4,16,128]{4,3,2,1,0:T(8,128)}, f32[8,24,4,16,128]{4,3,2,1,0:T(8,128)S(1)}, u32[]{:S(2)}) copy-start(f32[8,24,4,16,128]{4,3,2,1,0:T(8,128)S(1)} %brick_exchange.1) | copy-start | bytes 18874372

commit v2 on v1

--- a/solution.py
+++ b/solution.py
@@ -21,7 +21,7 @@
 
 MESH = pl.DeviceIdType.MESH
 PAD = 8
-CHUNK = 16
+CHUNK = BR
 TILE = 256
 
 
@@ -79,70 +79,108 @@
     )
 
 
-def exchange_kernel(owners, per_owner, src_ref, accel_ref, weight_ref, out_ref, send, send_sem, recv_sem):
+def exchange_kernel(
+    owners, per_owner, src_ref, ids_ref, accel_ref, weight_ref, main_out, side_out,
+    main, side, main_send, main_recv, side_send, side_recv,
+):
     me = lax.axis_index("yz")
     barrier = pltpu.get_barrier_semaphore()
     for k in range(1, owners):
         pl.semaphore_signal(
             barrier, inc=1, device_id={"yz": lax.rem(me + k, owners)}, device_id_type=MESH
         )
-    pl.semaphore_wait(barrier, owners - 1)
+    row_cells, col_cells = weight_ref.shape[1:]
+    row = lax.broadcasted_iota(jnp.int32, (row_cells, col_cells), 0)
+    lane = lax.broadcasted_iota(jnp.int32, (row_cells, col_cells), 1)
+    held = side_rows(per_owner)
 
     def pack(k, owner):
-        def one(p, carry):
+        def one(p, cols):
             slot = src_ref[owner * per_owner + p]
-            send[k, p, 0] = weight_ref[slot]
-            send[k, p, 1] = accel_ref[slot, 0]
-            send[k, p, 2] = accel_ref[slot, 1]
-            send[k, p, 3] = accel_ref[slot, 2]
-            return carry
-
-        lax.fori_loop(0, per_owner, one, 0)
-
+            root = jnp.sqrt(weight_ref[slot])
+            ax, ay = accel_ref[slot, 1], accel_ref[slot, 2]
+            px, py = root * ax, root * ay
+            s_up = jnp.where(row == 0, 0.0, pltpu.roll(root, 1, 0))
+            s_down = jnp.where(row == row_cells - 1, 0.0, pltpu.roll(root, row_cells - 1, 0))
+            s_left = jnp.where(lane == 0, 0.0, pltpu.roll(root, 1, 1))
+            s_right = jnp.where(lane == col_cells - 1, 0.0, pltpu.roll(root, col_cells - 1, 1))
+            p_up = jnp.where(row == 0, 0.0, pltpu.roll(px, 1, 0))
+            p_down = jnp.where(row == row_cells - 1, 0.0, pltpu.roll(px, row_cells - 1, 0))
+            p_left = jnp.where(lane == 0, 0.0, pltpu.roll(py, 1, 1))
+            p_right = jnp.where(lane == col_cells - 1, 0.0, pltpu.roll(py, col_cells - 1, 1))
+            total = p_up - p_down + p_left - p_right + ax * (s_up - s_down) + ay * (s_left - s_right)
+            main[k, p, 0] = root
+            main[k, p, 1] = accel_ref[slot, 0]
+            main[k, p, 2] = 0.5 * root * total
+            side[k, pl.ds(p, 1), :] = ax[0:1]
+            side[k, pl.ds(held + p, 1), :] = ax[row_cells - 1 : row_cells]
+            cols = jnp.where(lane == 2 * p, ay[:, 0:1], cols)
+            return jnp.where(lane == 2 * p + 1, ay[:, col_cells - 1 : col_cells], cols)
+
+        cols = lax.fori_loop(0, per_owner, one, jnp.zeros((row_cells, col_cells), jnp.float32))
+        side[k, 2 * held : 2 * held + row_cells, :] = cols
+        side[k, 2 * held + row_cells :, :] = ids_ref[owner]
+
+    side[...] = jnp.zeros_like(side)
     copies = []
     for k in range(1, owners):
         owner = lax.rem(me + k, owners)
         pack(k, owner)
-        copy = pltpu.make_async_remote_copy(
-            src_ref=send.at[k],
-            dst_ref=out_ref.at[me],
-            send_sem=send_sem.at[k],
-            recv_sem=recv_sem.at[k],
-            device_id={"yz": owner},
-            device_id_type=MESH,
-        )
+        if k == 1:
+            pl.semaphore_wait(barrier, owners - 1)
+        for src, dst, send, recv in (
+            (main, main_out, main_send, main_recv),
+            (side, side_out, side_send, side_recv),
+        ):
+            copy = pltpu.make_async_remote_copy(
+                src_ref=src.at[k],
+                dst_ref=dst.at[me],
+                send_sem=send.at[k],
+                recv_sem=recv.at[k],
+                device_id={"yz": owner},
+                device_id_type=MESH,
+            )
+            copy.start()
+            copies.append(copy)
+    pack(0, me)
+    own = [
+        pltpu.make_async_copy(main.at[0], main_out.at[me], main_send.at[0]),
+        pltpu.make_async_copy(side.at[0], side_out.at[me], side_send.at[0]),
+    ]
+    for copy in own:
         copy.start()
-        copies.append(copy)
-    pack(0, me)
-    own = pltpu.make_async_copy(send.at[0], out_ref.at[me], send_sem.at[0])
-    own.start()
-    own.wait()
+    for copy in own:
+        copy.wait()
     for copy in copies:
         copy.wait()
 
 
-def exchange(source, accel, weight, owners, per_owner):
+def side_rows(per_owner):
+    return -(-per_owner // 8) * 8
+
+
+def exchange(source, ids, accel, weight, owners, per_owner):
     slots, _, row_cells, col_cells = accel.shape
-    shape = (owners, per_owner, 4, row_cells, col_cells)
+    main_shape = (owners, per_owner, 3, row_cells, col_cells)
+    side_shape = (owners, 2 * side_rows(per_owner) + row_cells + 8, col_cells)
     return pl.pallas_call(
         functools.partial(exchange_kernel, owners, per_owner),
-        out_shape=jax.ShapeDtypeStruct(shape, jnp.float32),
-        in_specs=[
-            pl.BlockSpec(memory_space=pltpu.SMEM),
-            pl.BlockSpec(memory_space=pltpu.VMEM),
-            pl.BlockSpec(memory_space=pltpu.VMEM),
-        ],
-        out_specs=pl.BlockSpec(memory_space=pl.ANY),
+        out_shape=(
+            jax.ShapeDtypeStruct(main_shape, jnp.float32),
+            jax.ShapeDtypeStruct(side_shape, jnp.float32),
+        ),
+        in_specs=[pl.BlockSpec(memory_space=pltpu.SMEM)] + [pl.BlockSpec(memory_space=pltpu.VMEM)] * 3,
+        out_specs=(pl.BlockSpec(memory_space=pl.ANY), pl.BlockSpec(memory_space=pl.ANY)),
         scratch_shapes=[
-            pltpu.VMEM(shape, jnp.float32),
-            pltpu.SemaphoreType.DMA((owners,)),
-            pltpu.SemaphoreType.DMA((owners,)),
-        ],
+            pltpu.VMEM(main_shape, jnp.float32),
+            pltpu.VMEM(side_shape, jnp.float32),
+        ]
+        + [pltpu.SemaphoreType.DMA((owners,))] * 4,
         compiler_params=pltpu.CompilerParams(
             collective_id=0, has_side_effects=True, vmem_limit_bytes=40 * 2**20
         ),
         name="brick_exchange",
-    )(source, accel, weight)
+    )(source, ids, accel, weight)
 
 
 def split(value):
@@ -155,10 +193,10 @@
 
 
 def solver_kernel(
-    slabs, owners, rows, y_bricks,
-    anchor_ref, fluid_ref, bricks_ref, fwd_hbm, inv_hbm, table_x, table_xt, inverse_ref, ends_ref, couple_ref,
+    slabs, owners, rows, y_bricks, per_owner,
+    from_ref, place_ref, fluid_ref, main_ref, side_ref, fwd_hbm, inv_hbm, table_x, table_xt, inverse_ref, ends_ref, couple_ref,
     solution_ref, residual_ref,
-    fwd, inv, root, accel_x, accel_y, accel_z, fluid, diagonal, near_root, near_accel, near_t, t_pad,
+    fwd, inv, root, accel_x, accel_y, accel_z, source, fluid, diagonal, near_root, near_accel, near_t, t_pad,
     res_hl, spec, x_hl, update, image, edge, gathered, part, total_yz, total_gx,
     table_sem, near_sem, row_sem, t_sem, t_row_sem, edge_sem, yz_sem, gx_sem,
 ):
@@ -240,21 +278,36 @@
         def _():
             near[1] = jnp.zeros((rows, NY), jnp.float32)
 
+    held = side_rows(per_owner)
+    brick_row = lax.broadcasted_iota(jnp.int32, (BR, B), 0)
+    brick_lane = lax.broadcasted_iota(jnp.int32, (BR, B), 1)
+
     def place(b, carry):
-        slot = anchor_ref[b]
+        owner = from_ref[b]
+        p = place_ref[b]
         keep = fluid_ref[b]
         r0 = pl.multiple_of((b // y_bricks) * BR, BR)
         c0 = pl.multiple_of((b % y_bricks) * B, B)
         at = (pl.ds(r0, BR), pl.ds(c0, B))
         at_pad = (pl.ds(pl.multiple_of(r0 + PAD, PAD), BR), pl.ds(c0, B))
-        root[at_pad] = jnp.sqrt(bricks_ref[slot, 0] * keep)
-        accel_z[at] = bricks_ref[slot, 1] * keep
-        accel_x[at_pad] = bricks_ref[slot, 2] * keep
-        accel_y[at] = bricks_ref[slot, 3] * keep
+        root[at_pad] = main_ref[owner, p, 0] * keep
+        accel_z[at] = main_ref[owner, p, 1] * keep
+        source[at] = main_ref[owner, p, 2] * keep
+        top = side_ref[owner, pl.ds(p, 1), :]
+        bottom = side_ref[owner, pl.ds(held + p, 1), :]
+        cols = side_ref[owner, 2 * held : 2 * held + BR, :]
+        begin = jnp.sum(jnp.where(brick_lane == 2 * p, cols, 0.0), axis=1, keepdims=True)
+        end = jnp.sum(jnp.where(brick_lane == 2 * p + 1, cols, 0.0), axis=1, keepdims=True)
+        accel_x[at_pad] = keep * jnp.where(
+            brick_row == 0, top, jnp.where(brick_row == BR - 1, bottom, 0.0)
+        )
+        accel_y[at] = keep * jnp.where(
+            brick_lane == 0, begin, jnp.where(brick_lane == B - 1, end, 0.0)
+        )
         fluid[at] = jnp.full((BR, B), keep, jnp.float32)
         return carry
 
-    lax.fori_loop(0, rows // BR * y_bricks, place, 0)
+    lax.fori_loop(0, rows // BR * y_bricks, place, 0, unroll=2)
 
     pl.semaphore_wait(barrier, owners + slabs - 2)
     root_rows = root.at[pl.ds(PAD, rows)]
@@ -276,6 +329,7 @@
     for pair in near_pairs:
         wait_pair(pair, has_low, has_high)
 
+    row = lax.broadcasted_iota(jnp.int32, (CHUNK, NY), 0)
     lane = lax.broadcasted_iota(jnp.int32, (CHUNK, NY), 1)
 
     def left(value):
@@ -313,10 +367,12 @@
         s_left, s_right = left(s), right(s)
         s_low, s_high = near_root[0, at, :], near_root[1, at, :]
         az = accel_z[at, :]
-        total = px_up - px_down + ax * (s_up - s_down)
-        total = total + left(py) - right(py) + ay * (s_left - s_right)
+        total = jnp.where(row == 0, px_up + ax * s_up, 0.0)
+        total = total - jnp.where(row == CHUNK - 1, px_down + ax * s_down, 0.0)
+        total = total + jnp.where(lane % B == 0, left(py) + ay * s_left, 0.0)
+        total = total - jnp.where(lane % B == B - 1, right(py) + ay * s_right, 0.0)
         total = total + s_low * near_accel[0, at, :] - s_high * near_accel[1, at, :] + az * (s_low - s_high)
-        store_residual(at, 0.5 * s * total)
+        store_residual(at, source[at, :] + 0.5 * s * total)
         ring = s_up + s_down + s_left + s_right + s_low + s_high
         diagonal[at, :] = s * (shift_rate * s + ring) + (1.0 - fluid[at, :])
         return carry
@@ -409,8 +465,8 @@
 
         zero = jnp.zeros((CHUNK, NY), jnp.float32)
         energy, curve = lax.fori_loop(0, chunks, one, (zero, zero))
-        row = lax.broadcasted_iota(jnp.int32, (8, B), 0)
-        block = jnp.where(row < 4, jnp.sum(energy), jnp.sum(curve))
+        half = lax.broadcasted_iota(jnp.int32, (8, B), 0)
+        block = jnp.where(half < 4, jnp.sum(energy), jnp.sum(curve))
         for buf, sems, axis, count, index in (
             (total_yz, yz_sem, "yz", owners, z),
             (total_gx, gx_sem, "gx", slabs, g),
@@ -456,7 +512,7 @@
     lax.fori_loop(0, chunks, finish, 0)
 
 
-def solve(anchor, fluid, bricks, slabs, owners, rows, y_bricks):
+def solve(owner_of, place_of, fluid, main, side, slabs, owners, rows, y_bricks):
     tables = [jnp.asarray(t) for t in solver_tables(slabs, rows)]
     plane = (rows, NY)
     padded = (rows + 2 * PAD, NY)
@@ -467,15 +523,16 @@
     dma = pltpu.SemaphoreType.DMA
     out = jax.ShapeDtypeStruct((1,) + plane, f32)
     return pl.pallas_call(
-        functools.partial(solver_kernel, slabs, owners, rows, y_bricks),
+        functools.partial(solver_kernel, slabs, owners, rows, y_bricks, main.shape[1]),
         out_shape=(out, out),
-        in_specs=[smem, smem, vmem, hbm, hbm] + [vmem] * 5,
+        in_specs=[smem] * 3 + [vmem, vmem, hbm, hbm] + [vmem] * 5,
         out_specs=(vmem, vmem),
         scratch_shapes=[
             pltpu.VMEM((2, NY, NY), bf16),
             pltpu.VMEM((2, NY, NY), bf16),
             pltpu.VMEM(padded, f32),
             pltpu.VMEM(padded, f32),
+            pltpu.VMEM(plane, f32),
             pltpu.VMEM(plane, f32),
             pltpu.VMEM(plane, f32),
             pltpu.VMEM(plane, f32),
@@ -507,7 +564,7 @@
             collective_id=1, has_side_effects=True, vmem_limit_bytes=60 * 2**20
         ),
         name="pressure_solver",
-    )(anchor, fluid, bricks, *tables)
+    )(owner_of, place_of, fluid, main, side, *tables)
 
 
 def ranks_of(owners_of, owner_count):
@@ -523,7 +580,6 @@
     per_owner = 3 * slot_count // (2 * owner_count)
     rows = NX // slabs
     y_bricks = NY // B
-    me = lax.axis_index("yz")
     slots = jnp.arange(slot_count, dtype=jnp.int32)
 
     brick_ids = brick_slot[0]
@@ -533,18 +589,20 @@
     matches = target[None, :] == positions[:, None]
     source = jnp.sum(jnp.where(matches, slots[None, :], 0), axis=1)
 
-    all_ids = lax.all_gather(brick_ids, "yz")
-    mine = all_ids // slot_count == me
-    earlier = jnp.cumsum(mine.astype(jnp.int32), axis=1) - mine.astype(jnp.int32)
-    place_of = jnp.arange(owner_count, dtype=jnp.int32)[:, None] * per_owner + earlier
-    wanted = me * slot_count + slots
-    arrived = all_ids.reshape(-1)[None, :] == wanted[:, None]
-    anchor = jnp.sum(jnp.where(arrived, place_of.reshape(-1)[None, :], 0), axis=1)
-
-    bricks = exchange(source, camera_accel[0], camera_weight[0], owner_count, per_owner)
-    bricks = bricks.reshape((owner_count * per_owner,) + bricks.shape[2:])
+    found = jnp.sum(jnp.where(matches, 1 + brick_ids[None, :] % slot_count, 0), axis=1) - 1
+    ids = jnp.pad(
+        found.astype(jnp.float32).reshape(owner_count, 1, per_owner),
+        ((0, 0), (0, 7), (0, B - per_owner)),
+        constant_values=-1.0,
+    )
+    main, side = exchange(source, ids, camera_accel[0], camera_weight[0], owner_count, per_owner)
+    held_ids = side[:, -8, :per_owner].reshape(-1)
+    arrived = held_ids[None, :] == slots.astype(jnp.float32)[:, None]
+    anchor = jnp.sum(jnp.where(arrived, positions[None, :], 0), axis=1)
     fluid = (1 - brick_solid[0]).astype(jnp.float32)
-    return solve(anchor, fluid, bricks, slabs, owner_count, rows, y_bricks)
+    return solve(
+        anchor // per_owner, anchor % per_owner, fluid, main, side, slabs, owner_count, rows, y_bricks
+    )
 
 
 def solution(mesh):

time: 243 us -> 225 us (0.926)
  blocking collectives: 10.3 us -> 0 us
  Pallas kernels: 217 us -> 210 us
    pallas_call x1, Pallas kernels: 70.7 us -> 59.4 us  [exchange(): pl.pallas_call(functools.partial(exchange_kernel, owners, per_owner), out...]
    all_gather x1 -> x0, blocking collectives: 10.3 us -> none  [on_device(): all_ids = lax.all_gather(brick_ids, 'yz')]
    pallas_call x1, Pallas kernels: 147 us -> 151 us  [solve(): pl.pallas_call(functools.partial(solver_kernel, slabs, owners, rows, y_br...]
    unnamed x8 -> x10, local copies, waits for them, and re-layouts: 10.4 us -> 9.84 us
where the time goes in v2:
time: 225 us
  Pallas kernels  210 us (93%)
  local copies, waits for them, and re-layouts  10 us (4%)
  other arithmetic  3.82 us (2%)
    pallas_call x1, Pallas kernels, solve(): pl.pallas_call(functools.partial(solver_kernel, slabs, owners, rows, y_br...  151 us
    pallas_call x1, Pallas kernels, exchange(): pl.pallas_call(functools.partial(exchange_kernel, owners, per_owner), out...  59.4 us
    unnamed x10, local copies, waits for them, and re-layouts  9.84 us

profile of v2, /device:TPU:0, one launch (start us, length us, event | category | flops | bytes accessed | tf_op | source)
XLA Modules:
  0.0 224.9 jit_solution(8174107606017389934)
XLA Ops:
  0.6 0.7 and_select_fusion.3
  1.3 1.2 convert_bitcast_fusion.fluid_ref
  2.5 0.1 fusion
  2.6 0.2 reduce_window_sum.11
  2.7 0.2 select_reduce_fusion.3
  2.9 0.7 fusion.3
  3.6 0.2 select_reduce_fusion.1
  3.7 0.1 convert_element_type.30
  3.8 0.0 copy-start.1
  3.9 1.9 copy-done.1
  5.7 0.0 copy-start.2
  5.7 1.2 copy-done.2
  7.0 59.4 %brick_exchange.1 = (f32[8,24,3,16,128]{4,3,2,1,0:T(8,128)S(1)}, f32[8,72,128]{2,1,0:T(8,128)S(1)}) custom-call(s32[192]{0:T(256)S(1)} %get-tuple-element.7.src_ref, f32[8,8,128]{2,1,0:T(8,128)S(1)} %pad.4.ids_ref, f32[128,3,16,128]{3,2,1,0:T(8,128)S(1)} %bitcast.20, f32[128,16,128]{2,1,0:T(8,128)S(1)} %bitcast.21), custom_call_target="tpu_custom_call" | custom-call | tf_op jit(solution)/shard_map/brick_exchange/pallas_call | solution.py:166
  66.4 0.0 copy-start
  66.4 2.1 copy-done
  68.5 0.0 copy-start.3
  68.5 0.1 eq.54
  68.6 0.1 select_reduce_fusion
  68.7 0.6 and_select_fusion
  69.3 0.0 copy-done.3
  69.3 151.0 %pressure_solver.1 = (f32[1,256,1024]{2,1,0:T(8,128)}, f32[1,256,1024]{2,1,0:T(8,128)}) custom-call(s32[128]{0:T(128)} %get-tuple-element.9.from_ref, s32[128]{0:T(128)} %get-tuple-element.8.place_ref, f32[128]{0:T(128)} %convert_bitcast_fusion.fluid_ref, f32[8,24,3,16,128]{4,3,2,1,0:T(8,128)} %copy-done, f32[8,72,128]{2,1,0:T(8,128)} %copy-done.3, ...), custom_call_target="tpu_custom_call" | custom-call | tf_op jit(solution)/shard_map/pressure_solver/pallas_call | solution.py:525
  220.3 2.3 %copy.15 = f32[1,256,1024]{2,1,0:T(8,128)} copy(f32[1,256,1024]{2,1,0:T(8,128)} %get-tuple-element.14) | data formatting | bytes 2097152
  222.6 2.3 %copy.16 = f32[1,256,1024]{2,1,0:T(8,128)} copy(f32[1,256,1024]{2,1,0:T(8,128)} %get-tuple-element.15) | data formatting | bytes 2097152
  (4 shorter events, 0.0 us)
Async XLA Ops:
  3.8 1.9 copy-start.1
  5.7 1.2 copy-start.2
  66.4 2.1 copy-start
  68.5 0.8 copy-start.3

commit v3 on v2

--- a/solution.py
+++ b/solution.py
@@ -197,7 +197,7 @@
     from_ref, place_ref, fluid_ref, main_ref, side_ref, fwd_hbm, inv_hbm, table_x, table_xt, inverse_ref, ends_ref, couple_ref,
     solution_ref, residual_ref,
     fwd, inv, root, accel_x, accel_y, accel_z, source, fluid, diagonal, near_root, near_accel, near_t, t_pad,
-    res_hl, spec, x_hl, update, image, edge, gathered, part, total_yz, total_gx,
+    res_hl, spec, x_hl, update, image, edge, gathered, part, total_yz, total_gx, relay,
     table_sem, near_sem, row_sem, t_sem, t_row_sem, edge_sem, yz_sem, gx_sem,
 ):
     g = lax.axis_index("gx")
@@ -224,10 +224,70 @@
             device_id=device, device_id_type=MESH,
         )
 
-    def plane_copies(src, near, sems):
-        up = remote(src, near.at[0], sems.at[0], {"yz": jnp.minimum(z + 1, owners - 1)})
-        down = remote(src, near.at[1], sems.at[1], {"yz": jnp.maximum(z - 1, 0)})
-        return up, down
+    half = rows // 2
+    middle = owners // 2
+    via = (0, owners - 1)
+    tiles = NY // TILE
+
+    class Piece:
+        def __init__(self, src, near, held, sems):
+            parts = [pl.ds(0, half), pl.ds(half, half)]
+
+            def copy(src, dst, send, recv, device):
+                return pltpu.make_async_remote_copy(
+                    src_ref=src, dst_ref=dst, send_sem=sems.at[send], recv_sem=sems.at[recv],
+                    device_id={"yz": device}, device_id_type=MESH,
+                )
+
+            self.up = copy(src, near.at[0], 0, 1, jnp.minimum(z + 1, owners - 1))
+            self.down = copy(src, near.at[1], 2, 3, jnp.maximum(z - 1, 0))
+            self.out = [
+                [copy(src.at[parts[h]], held.at[d], 4 + h, 6 + d, via[h]) for h in range(2)]
+                for d in range(2)
+            ]
+            self.on = [
+                [copy(held.at[d], near.at[d, parts[h]], 8 + d, 10 + h, middle - d) for h in range(2)]
+                for d in range(2)
+            ]
+
+        def start(self):
+            pl.when((z < owners - 1) & (z != middle - 1))(self.up.start)
+            pl.when((z > 0) & (z != middle))(self.down.start)
+            for d in range(2):
+                for h in range(2):
+                    pl.when(z == middle - 1 + d)(self.out[d][h].start)
+
+        def forward(self):
+            for h in range(2):
+                @pl.when(z == via[h])
+                def _():
+                    for d in range(2):
+                        self.out[d][h].wait_recv()
+                        self.on[d][h].start()
+
+        def wait(self):
+            @pl.when((z < owners - 1) & (z != middle - 1))
+            def _():
+                self.up.wait_send()
+                self.down.wait_recv()
+
+            @pl.when((z > 0) & (z != middle))
+            def _():
+                self.down.wait_send()
+                self.up.wait_recv()
+
+            for d in range(2):
+                @pl.when(z == middle - 1 + d)
+                def _():
+                    for h in range(2):
+                        self.out[d][h].wait_send()
+                        self.on[1 - d][h].wait_recv()
+
+            for h in range(2):
+                @pl.when(z == via[h])
+                def _():
+                    for d in range(2):
+                        self.on[d][h].wait_send()
 
     def row_copies(buf, sems):
         after = remote(
@@ -279,10 +339,12 @@
             near[1] = jnp.zeros((rows, NY), jnp.float32)
 
     held = side_rows(per_owner)
+    per_tile = TILE // B
     brick_row = lax.broadcasted_iota(jnp.int32, (BR, B), 0)
     brick_lane = lax.broadcasted_iota(jnp.int32, (BR, B), 1)
 
-    def place(b, carry):
+    def place(first, n, carry):
+        b = (n // per_tile) * y_bricks + first + n % per_tile
         owner = from_ref[b]
         p = place_ref[b]
         keep = fluid_ref[b]
@@ -307,27 +369,32 @@
         fluid[at] = jnp.full((BR, B), keep, jnp.float32)
         return carry
 
-    lax.fori_loop(0, rows // BR * y_bricks, place, 0, unroll=2)
-
-    pl.semaphore_wait(barrier, owners + slabs - 2)
-    root_rows = root.at[pl.ds(PAD, rows)]
-    near_pairs = [
-        plane_copies(root_rows, near_root, near_sem.at[0]),
-        plane_copies(accel_z, near_accel, near_sem.at[1]),
-    ]
+    pieces = []
+    for j in range(tiles):
+        lax.fori_loop(
+            0, rows // BR * per_tile, functools.partial(place, j * per_tile), 0, unroll=2
+        )
+        if j == 0:
+            pl.semaphore_wait(barrier, owners + slabs - 2)
+        at = pl.ds(j * TILE, TILE)
+        pair = [
+            Piece(root.at[pl.ds(PAD, rows), at], near_root.at[:, :, at], relay.at[j], near_sem.at[0, j]),
+            Piece(accel_z.at[:, at], near_accel.at[:, :, at], relay.at[tiles + j], near_sem.at[1, j]),
+        ]
+        for piece in pair:
+            piece.start()
+        pieces.append(pair)
     row_pairs = [row_copies(root, row_sem.at[0]), row_copies(accel_x, row_sem.at[1])]
     for pair in row_pairs:
         start_pair(pair, has_next, has_prev)
-    for pair in near_pairs:
-        start_pair(pair, has_high, has_low)
     for buf in (root, accel_x, t_pad.at[0], t_pad.at[1]):
         clear_rows(buf)
+    for piece in pieces[0]:
+        piece.forward()
     for buf in (near_root, near_accel, near_t.at[0], near_t.at[1]):
         clear_planes(buf)
     for pair in row_pairs:
         wait_pair(pair, has_prev, has_next)
-    for pair in near_pairs:
-        wait_pair(pair, has_low, has_high)
 
     row = lax.broadcasted_iota(jnp.int32, (CHUNK, NY), 0)
     lane = lax.broadcasted_iota(jnp.int32, (CHUNK, NY), 1)
@@ -349,11 +416,11 @@
             wide[PAD + 1 : PAD + 1 + CHUNK],
         )
 
-    def store_residual(at, value):
-        residual_ref[0, at, :] = value
+    def store_residual(at, cols, value):
+        residual_ref[0, at, cols] = value
         high, low = split(value)
-        res_hl[0, at, :] = high
-        res_hl[1, at, :] = low
+        res_hl[0, at, cols] = high
+        res_hl[1, at, cols] = low
 
     def prepare(i, carry):
         at, wide_at = at_chunk(i)
@@ -365,24 +432,34 @@
         ay = accel_y[at, :]
         py = s * ay
         s_left, s_right = left(s), right(s)
-        s_low, s_high = near_root[0, at, :], near_root[1, at, :]
-        az = accel_z[at, :]
         total = jnp.where(row == 0, px_up + ax * s_up, 0.0)
         total = total - jnp.where(row == CHUNK - 1, px_down + ax * s_down, 0.0)
         total = total + jnp.where(lane % B == 0, left(py) + ay * s_left, 0.0)
         total = total - jnp.where(lane % B == B - 1, right(py) + ay * s_right, 0.0)
-        total = total + s_low * near_accel[0, at, :] - s_high * near_accel[1, at, :] + az * (s_low - s_high)
-        store_residual(at, source[at, :] + 0.5 * s * total)
-        ring = s_up + s_down + s_left + s_right + s_low + s_high
+        source[at, :] = source[at, :] + 0.5 * s * total
+        ring = s_up + s_down + s_left + s_right
         diagonal[at, :] = s * (shift_rate * s + ring) + (1.0 - fluid[at, :])
         return carry
 
     chunks = rows // CHUNK
     lax.fori_loop(0, chunks, prepare, 0)
+    for pair in pieces[1:]:
+        for piece in pair:
+            piece.forward()
     for copy in table_copies:
         copy.wait()
 
-    tiles = NY // TILE
+    every = pl.ds(0, NY)
+
+    def add_planes(cols, i, carry):
+        at, _ = at_chunk(i)
+        s = root[pl.ds(pl.multiple_of(i * CHUNK + PAD, PAD), CHUNK), cols]
+        s_low, s_high = near_root[0, at, cols], near_root[1, at, cols]
+        total = s_low * near_accel[0, at, cols] - s_high * near_accel[1, at, cols]
+        total = total + accel_z[at, cols] * (s_low - s_high)
+        store_residual(at, cols, source[at, cols] + 0.5 * s * total)
+        diagonal[at, cols] = diagonal[at, cols] + s * (s_low + s_high)
+        return carry
 
     def three(left_hl, right_hl):
         lh, ll = left_hl
@@ -392,11 +469,23 @@
     def tile_at(j):
         return pl.ds(pl.multiple_of(j * TILE, TILE), TILE)
 
+    def accumulate(j):
+        cols = pl.ds(j * TILE, TILE)
+
+        def one(k, carry):
+            at = tile_at(k)
+            lines = three((res_hl[0, :, cols], res_hl[1, :, cols]), (fwd[0, cols, at], fwd[1, cols, at]))
+            if j:
+                lines = spec[:, at] + lines
+            spec[:, at] = lines
+            return carry
+
+        lax.fori_loop(0, tiles, one, 0)
+
     def precondition(it):
         def forward(j, carry):
             at = tile_at(j)
-            lines = three((res_hl[0], res_hl[1]), (fwd[0, :, at], fwd[1, :, at]))
-            modes = three((table_x[0], table_x[1]), split(lines)) * inverse_ref[:, at]
+            modes = three((table_x[0], table_x[1]), split(spec[:, at])) * inverse_ref[:, at]
             spec[:, at] = modes
             edge[it, 0:1, at] = jnp.sum(modes * ends_ref[:, 0:1], axis=0, keepdims=True)
             edge[it, 1:2, at] = jnp.sum(modes * ends_ref[:, B : B + 1], axis=0, keepdims=True)
@@ -440,33 +529,49 @@
             out = three((x_hl[0], x_hl[1]), (inv[0, :, at], inv[1, :, at])) * fluid[:, at]
             update[it, :, at] = out
             t_pad[it, pl.ds(PAD, rows), at] = out * root[pl.ds(PAD, rows), at]
-            pair = plane_copies(
-                t_pad.at[it, pl.ds(PAD, rows), at], near_t.at[it, :, :, at], t_sem.at[it, j]
+            piece = Piece(
+                t_pad.at[it, pl.ds(PAD, rows), at], near_t.at[it, :, :, at],
+                relay.at[(2 + it) * tiles + j], t_sem.at[it, j],
             )
-            start_pair(pair, has_high, has_low)
-            pairs.append(pair)
+            piece.start()
+            pairs.append(piece)
         rim = row_copies(t_pad.at[it], t_row_sem.at[it])
         start_pair(rim, has_next, has_prev)
+        pairs[0].forward()
         wait_pair(rim, has_prev, has_next)
-        for pair in pairs:
-            wait_pair(pair, has_low, has_high)
-
-    def operate(it):
-        def one(i, carry):
-            energy, curve = carry
+        return pairs
+
+    def operate(it, pairs):
+        def within(i, carry):
             at, wide_at = at_chunk(i)
             t_up, t, t_down = shifts(t_pad[it, wide_at, :])
             _, s, _ = shifts(root[wide_at, :])
-            near = t_up + t_down + left(t) + right(t) + near_t[it, 0, at, :] + near_t[it, 1, at, :]
-            u = update[it, at, :]
-            out = diagonal[at, :] * u - s * near
-            image[it, at, :] = out
-            return energy + u * residual_ref[0, at, :], curve + u * out
-
-        zero = jnp.zeros((CHUNK, NY), jnp.float32)
-        energy, curve = lax.fori_loop(0, chunks, one, (zero, zero))
-        half = lax.broadcasted_iota(jnp.int32, (8, B), 0)
-        block = jnp.where(half < 4, jnp.sum(energy), jnp.sum(curve))
+            near = t_up + t_down + left(t) + right(t)
+            image[it, at, :] = diagonal[at, :] * update[it, at, :] - s * near
+            return carry
+
+        lax.fori_loop(0, chunks, within, 0)
+        for piece in pairs[1:]:
+            piece.forward()
+
+        def across(cols, i, carry):
+            energy, curve = carry
+            at, _ = at_chunk(i)
+            s = root[pl.ds(pl.multiple_of(i * CHUNK + PAD, PAD), CHUNK), cols]
+            u = update[it, at, cols]
+            out = image[it, at, cols] - s * (near_t[it, 0, at, cols] + near_t[it, 1, at, cols])
+            image[it, at, cols] = out
+            return energy + u * residual_ref[0, at, cols], curve + u * out
+
+        zero = jnp.zeros((CHUNK, TILE), jnp.float32)
+        energy, curve = zero, zero
+        for j in range(tiles):
+            pairs[j].wait()
+            energy, curve = lax.fori_loop(
+                0, chunks, functools.partial(across, pl.ds(j * TILE, TILE)), (energy, curve)
+            )
+        part_row = lax.broadcasted_iota(jnp.int32, (8, B), 0)
+        block = jnp.where(part_row < 4, jnp.sum(energy), jnp.sum(curve))
         for buf, sems, axis, count, index in (
             (total_yz, yz_sem, "yz", owners, z),
             (total_gx, gx_sem, "gx", slabs, g),
@@ -485,18 +590,23 @@
                 block = block + buf[it, k]
         return block[0:1, 0:1], block[4:5, 0:1]
 
-    precondition(0)
-    energy_now, curvature = operate(0)
+    for j in range(tiles):
+        for piece in pieces[j]:
+            piece.wait()
+        lax.fori_loop(0, chunks, functools.partial(add_planes, pl.ds(j * TILE, TILE)), 0)
+        accumulate(j)
+    energy_now, curvature = operate(0, precondition(0))
     step_now = energy_now / curvature
 
     def advance(i, carry):
         at, _ = at_chunk(i)
-        store_residual(at, residual_ref[0, at, :] - step_now * image[0, at, :])
+        store_residual(at, every, residual_ref[0, at, :] - step_now * image[0, at, :])
         return carry
 
     lax.fori_loop(0, chunks, advance, 0)
-    precondition(1)
-    energy_next, curvature = operate(1)
+    for j in range(tiles):
+        accumulate(j)
+    energy_next, curvature = operate(1, precondition(1))
     beta = energy_next / energy_now
     step_next = energy_next / (curvature - beta * energy_next / step_now)
 
@@ -551,10 +661,11 @@
             pltpu.VMEM((8, NY), f32),
             pltpu.VMEM((ITERS, owners, 8, B), f32),
             pltpu.VMEM((ITERS, slabs, 8, B), f32),
+            pltpu.VMEM(((2 + ITERS) * (NY // TILE), 2, rows // 2, TILE), f32),
             dma((2,)),
+            dma((2, NY // TILE, 12)),
             dma((2, 2, 2)),
-            dma((2, 2, 2)),
-            dma((ITERS, NY // TILE, 2, 2)),
+            dma((ITERS, NY // TILE, 12)),
             dma((ITERS, 2, 2)),
             dma((ITERS, slabs, 2)),
             dma((ITERS, owners, 2)),

time: 225 us -> 198 us (0.88)
  Pallas kernels: 210 us -> 183 us
    pallas_call x1, Pallas kernels: 151 us -> 123 us  [solve(): pl.pallas_call(functools.partial(solver_kernel, slabs, owners, rows, y_br...]
where the time goes in v3:
time: 198 us; the launch traced here: 197 us
  Pallas kernels  183 us (92%)
  local copies, waits for them, and re-layouts  10 us (5%)
  other arithmetic  3.82 us (2%)
    pallas_call x1, Pallas kernels, solve(): pl.pallas_call(functools.partial(solver_kernel, slabs, owners, rows, y_br...  123 us
    pallas_call x1, Pallas kernels, exchange(): pl.pallas_call(functools.partial(exchange_kernel, owners, per_owner), out...  59.4 us
    unnamed x10, local copies, waits for them, and re-layouts  9.84 us

profile of v3, /device:TPU:0, one launch (start us, length us, event | category | flops | bytes accessed | tf_op | source)
XLA Modules:
  0.0 197.4 jit_solution(13415817536925352479)
XLA Ops:
  0.6 0.7 and_select_fusion.3
  1.3 1.2 convert_bitcast_fusion.fluid_ref
  2.5 0.1 fusion
  2.6 0.2 reduce_window_sum.11
  2.7 0.2 select_reduce_fusion.3
  2.9 0.7 fusion.3
  3.6 0.2 select_reduce_fusion.1
  3.7 0.1 convert_element_type.30
  3.8 0.0 copy-start.1
  3.9 1.9 copy-done.1
  5.7 0.0 copy-start.2
  5.7 1.2 copy-done.2
  7.0 59.4 %brick_exchange.1 = (f32[8,24,3,16,128]{4,3,2,1,0:T(8,128)S(1)}, f32[8,72,128]{2,1,0:T(8,128)S(1)}) custom-call(s32[192]{0:T(256)S(1)} %get-tuple-element.7.src_ref, f32[8,8,128]{2,1,0:T(8,128)S(1)} %pad.4.ids_ref, f32[128,3,16,128]{3,2,1,0:T(8,128)S(1)} %bitcast.20, f32[128,16,128]{2,1,0:T(8,128)S(1)} %bitcast.21), custom_call_target="tpu_custom_call" | custom-call | tf_op jit(solution)/shard_map/brick_exchange/pallas_call | solution.py:166
  66.4 0.0 copy-start
  66.4 2.1 %copy-done = f32[8,24,3,16,128]{4,3,2,1,0:T(8,128)} copy-done((f32[8,24,3,16,128]{4,3,2,1,0:T(8,128)}, f32[8,24,3,16,128]{4,3,2,1,0:T(8,128)S(1)}, u32[]{:S(2)}) %copy-start) | copy-done | bytes 4718616
  68.5 0.0 copy-start.3
  68.5 0.1 eq.54
  68.6 0.1 select_reduce_fusion
  68.7 0.6 and_select_fusion
  69.3 0.0 copy-done.3
  69.3 123.4 %pressure_solver.1 = (f32[1,256,1024]{2,1,0:T(8,128)}, f32[1,256,1024]{2,1,0:T(8,128)}) custom-call(s32[128]{0:T(128)} %get-tuple-element.9.from_ref, s32[128]{0:T(128)} %get-tuple-element.8.place_ref, f32[128]{0:T(128)} %convert_bitcast_fusion.fluid_ref, f32[8,24,3,16,128]{4,3,2,1,0:T(8,128)} %copy-done, f32[8,72,128]{2,1,0:T(8,128)} %copy-done.3, ...), custom_call_target="tpu_custom_call" | custom-call | tf_op jit(solution)/shard_map/pressure_solver/pallas_call | solution.py:635
  192.7 2.3 %copy.15 = f32[1,256,1024]{2,1,0:T(8,128)} copy(f32[1,256,1024]{2,1,0:T(8,128)} %get-tuple-element.14) | data formatting | bytes 2097152
  195.1 2.3 %copy.16 = f32[1,256,1024]{2,1,0:T(8,128)} copy(f32[1,256,1024]{2,1,0:T(8,128)} %get-tuple-element.15) | data formatting | bytes 2097152
  (4 shorter events, 0.0 us)
Async XLA Ops:
  3.8 1.9 copy-start.1
  5.7 1.2 copy-start.2
  66.4 2.1 %copy-start = (f32[8,24,3,16,128]{4,3,2,1,0:T(8,128)}, f32[8,24,3,16,128]{4,3,2,1,0:T(8,128)S(1)}, u32[]{:S(2)}) copy-start(f32[8,24,3,16,128]{4,3,2,1,0:T(8,128)S(1)} %get-tuple-element.5.main_ref) | copy-start | bytes 14155780
  68.5 0.8 copy-start.3

commit v4 on v3

--- a/solution.py
+++ b/solution.py
@@ -23,6 +23,7 @@
 PAD = 8
 CHUNK = BR
 TILE = 256
+WIDE = 512
 
 
 def cosine_table(length):
@@ -79,6 +80,20 @@
     )
 
 
+def partner(me, k, owners):
+    total, bit = 0, 1
+    while bit < owners:
+        digit = (me // bit) % 2
+        total = total + bit * (1 - digit if k & bit else digit)
+        bit *= 2
+    return total
+
+
+def partner_order(owners):
+    far = [k for k in range(owners - 1, 1, -1) if k % 2 == 0]
+    return far + [k + 1 for k in far] + [1]
+
+
 def exchange_kernel(
     owners, per_owner, src_ref, ids_ref, accel_ref, weight_ref, main_out, side_out,
     main, side, main_send, main_recv, side_send, side_recv,
@@ -123,10 +138,10 @@
 
     side[...] = jnp.zeros_like(side)
     copies = []
-    for k in range(1, owners):
-        owner = lax.rem(me + k, owners)
+    for count, k in enumerate(partner_order(owners)):
+        owner = partner(me, k, owners)
         pack(k, owner)
-        if k == 1:
+        if count == 0:
             pl.semaphore_wait(barrier, owners - 1)
         for src, dst, send, recv in (
             (main, main_out, main_send, main_recv),
@@ -467,7 +482,7 @@
         return dot32(lh, rh) + dot32(lh, rl) + dot32(ll, rh)
 
     def tile_at(j):
-        return pl.ds(pl.multiple_of(j * TILE, TILE), TILE)
+        return pl.ds(pl.multiple_of(j * WIDE, WIDE), WIDE)
 
     def accumulate(j):
         cols = pl.ds(j * TILE, TILE)
@@ -480,19 +495,23 @@
             spec[:, at] = lines
             return carry
 
-        lax.fori_loop(0, tiles, one, 0)
+        lax.fori_loop(0, NY // WIDE, one, 0)
 
     def precondition(it):
         def forward(j, carry):
             at = tile_at(j)
-            modes = three((table_x[0], table_x[1]), split(spec[:, at])) * inverse_ref[:, at]
+            if it:
+                lines = three((res_hl[0], res_hl[1]), (fwd[0, :, at], fwd[1, :, at]))
+            else:
+                lines = spec[:, at]
+            modes = three((table_x[0], table_x[1]), split(lines)) * inverse_ref[:, at]
             spec[:, at] = modes
             edge[it, 0:1, at] = jnp.sum(modes * ends_ref[:, 0:1], axis=0, keepdims=True)
             edge[it, 1:2, at] = jnp.sum(modes * ends_ref[:, B : B + 1], axis=0, keepdims=True)
             return carry
 
         edge[it] = jnp.zeros((8, NY), jnp.float32)
-        lax.fori_loop(0, tiles, forward, 0)
+        lax.fori_loop(0, NY // WIDE, forward, 0)
         copies = [
             remote(edge.at[it], gathered.at[it, g], edge_sem.at[it, k], {"gx": lax.rem(g + k, slabs)})
             for k in range(1, slabs)
@@ -522,7 +541,7 @@
             x_hl[1, :, at] = low
             return carry
 
-        lax.fori_loop(0, tiles, back_x, 0)
+        lax.fori_loop(0, NY // WIDE, back_x, 0)
         pairs = []
         for j in range(tiles):
             at = pl.ds(j * TILE, TILE)
@@ -604,8 +623,6 @@
         return carry
 
     lax.fori_loop(0, chunks, advance, 0)
-    for j in range(tiles):
-        accumulate(j)
     energy_next, curvature = operate(1, precondition(1))
     beta = energy_next / energy_now
     step_next = energy_next / (curvature - beta * energy_next / step_now)

time: 198 us -> 191 us (0.965)
  Pallas kernels: 183 us -> 176 us
    pallas_call x1, Pallas kernels: 123 us -> 115 us  [solve(): pl.pallas_call(functools.partial(solver_kernel, slabs, owners, rows, y_br...]
where the time goes in v4:
time: 191 us; the launch traced here: 190 us
  Pallas kernels  176 us (92%)
  local copies, waits for them, and re-layouts  10 us (5%)
  other arithmetic  3.82 us (2%)
    pallas_call x1, Pallas kernels, solve(): pl.pallas_call(functools.partial(solver_kernel, slabs, owners, rows, y_br...  115 us
    pallas_call x1, Pallas kernels, exchange(): pl.pallas_call(functools.partial(exchange_kernel, owners, per_owner), out...  61.3 us
    unnamed x10, local copies, waits for them, and re-layouts  9.84 us

profile of v4, /device:TPU:0, one launch (start us, length us, event | category | flops | bytes accessed | tf_op | source)
XLA Modules:
  0.0 190.4 jit_solution(7803251276171706933)
XLA Ops:
  0.6 0.7 and_select_fusion.3
  1.3 1.2 convert_bitcast_fusion.fluid_ref
  2.5 0.1 fusion
  2.6 0.2 reduce_window_sum.11
  2.7 0.2 select_reduce_fusion.3
  2.9 0.7 fusion.3
  3.6 0.2 select_reduce_fusion.1
  3.7 0.1 convert_element_type.30
  3.8 0.0 copy-start.1
  3.9 1.9 copy-done.1
  5.7 0.0 copy-start.2
  5.7 1.2 copy-done.2
  7.0 61.3 %brick_exchange.1 = (f32[8,24,3,16,128]{4,3,2,1,0:T(8,128)S(1)}, f32[8,72,128]{2,1,0:T(8,128)S(1)}) custom-call(s32[192]{0:T(256)S(1)} %get-tuple-element.7.src_ref, f32[8,8,128]{2,1,0:T(8,128)S(1)} %pad.4.ids_ref, f32[128,3,16,128]{3,2,1,0:T(8,128)S(1)} %bitcast.20, f32[128,16,128]{2,1,0:T(8,128)S(1)} %bitcast.21), custom_call_target="tpu_custom_call" | custom-call | tf_op jit(solution)/shard_map/brick_exchange/pallas_call | solution.py:181
  68.2 0.0 copy-start
  68.3 2.1 %copy-done = f32[8,24,3,16,128]{4,3,2,1,0:T(8,128)} copy-done((f32[8,24,3,16,128]{4,3,2,1,0:T(8,128)}, f32[8,24,3,16,128]{4,3,2,1,0:T(8,128)S(1)}, u32[]{:S(2)}) %copy-start) | copy-done | bytes 4718616
  70.4 0.0 copy-start.3
  70.4 0.1 eq.54
  70.5 0.1 select_reduce_fusion
  70.6 0.6 and_select_fusion
  71.2 0.0 copy-done.3
  71.2 114.6 %pressure_solver.1 = (f32[1,256,1024]{2,1,0:T(8,128)}, f32[1,256,1024]{2,1,0:T(8,128)}) custom-call(s32[128]{0:T(128)} %get-tuple-element.9.from_ref, s32[128]{0:T(128)} %get-tuple-element.8.place_ref, f32[128]{0:T(128)} %convert_bitcast_fusion.fluid_ref, f32[8,24,3,16,128]{4,3,2,1,0:T(8,128)} %copy-done, f32[8,72,128]{2,1,0:T(8,128)} %copy-done.3, ...), custom_call_target="tpu_custom_call" | custom-call | tf_op jit(solution)/shard_map/pressure_solver/pallas_call | solution.py:652
  185.8 2.3 %copy.15 = f32[1,256,1024]{2,1,0:T(8,128)} copy(f32[1,256,1024]{2,1,0:T(8,128)} %get-tuple-element.14) | data formatting | bytes 2097152
  188.1 2.3 %copy.16 = f32[1,256,1024]{2,1,0:T(8,128)} copy(f32[1,256,1024]{2,1,0:T(8,128)} %get-tuple-element.15) | data formatting | bytes 2097152
  (4 shorter events, 0.0 us)
Async XLA Ops:
  3.8 1.9 copy-start.1
  5.7 1.2 copy-start.2
  68.2 2.1 %copy-start = (f32[8,24,3,16,128]{4,3,2,1,0:T(8,128)}, f32[8,24,3,16,128]{4,3,2,1,0:T(8,128)S(1)}, u32[]{:S(2)}) copy-start(f32[8,24,3,16,128]{4,3,2,1,0:T(8,128)S(1)} %get-tuple-element.5.main_ref) | copy-start | bytes 14155780
  70.4 0.8 copy-start.3

commit v5 on v4

--- a/solution.py
+++ b/solution.py
@@ -23,7 +23,7 @@
 PAD = 8
 CHUNK = BR
 TILE = 256
-WIDE = 512
+WIDE = 1024
 
 
 def cosine_table(length):
@@ -689,10 +689,29 @@
             dma((ITERS, slabs, 2)),
         ],
         compiler_params=pltpu.CompilerParams(
-            collective_id=1, has_side_effects=True, vmem_limit_bytes=60 * 2**20
+            collective_id=1, has_side_effects=True, vmem_limit_bytes=45 * 2**20
         ),
         name="pressure_solver",
     )(owner_of, place_of, fluid, main, side, *tables)
+
+
+def deliver_kernel(solution_in, residual_in, solution_ref, residual_ref):
+    solution_ref[...] = solution_in[...]
+    residual_ref[...] = residual_in[...]
+
+
+def deliver(values):
+    _, rows, cols = values[0].shape
+    steps = 4
+    block = pl.BlockSpec((1, rows // steps, cols), lambda i: (0, i, 0))
+    return pl.pallas_call(
+        deliver_kernel,
+        grid=(steps,),
+        out_shape=tuple(jax.ShapeDtypeStruct(v.shape, v.dtype) for v in values),
+        in_specs=[block, block],
+        out_specs=(block, block),
+        name="deliver",
+    )(*values)
 
 
 def ranks_of(owners_of, owner_count):
@@ -728,9 +747,10 @@
     arrived = held_ids[None, :] == slots.astype(jnp.float32)[:, None]
     anchor = jnp.sum(jnp.where(arrived, positions[None, :], 0), axis=1)
     fluid = (1 - brick_solid[0]).astype(jnp.float32)
-    return solve(
+    values = solve(
         anchor // per_owner, anchor % per_owner, fluid, main, side, slabs, owner_count, rows, y_bricks
     )
+    return deliver(values)
 
 
 def solution(mesh):

time: 191 us -> 189 us (0.990)
    pallas_call x1, Pallas kernels: 115 us -> 111 us  [solve(): pl.pallas_call(functools.partial(solver_kernel, slabs, owners, rows, y_br...]
    pallas_call x0 -> x1, Pallas kernels: none -> 3.74 us  [deliver(): pl.pallas_call(deliver_kernel, grid=(steps,), out_shape=tuple((jax.ShapeD...]
    unnamed x10 -> x22, local copies, waits for them, and re-layouts: 9.84 us -> 9.45 us
where the time goes in v5:
time: 189 us
  Pallas kernels  176 us (93%)
  local copies, waits for them, and re-layouts  9.64 us (5%)
  other arithmetic  2.75 us (1%)
    pallas_call x1, Pallas kernels, solve(): pl.pallas_call(functools.partial(solver_kernel, slabs, owners, rows, y_br...  111 us
    pallas_call x1, Pallas kernels, exchange(): pl.pallas_call(functools.partial(exchange_kernel, owners, per_owner), out...  61.3 us
    unnamed x22, local copies, waits for them, and re-layouts  9.45 us

profile of v5, /device:TPU:0, one launch (start us, length us, event | category | flops | bytes accessed | tf_op | source)
XLA Modules:
  0.0 189.0 jit_solution(4042830730330581423)
XLA Ops:
  0.6 0.0 copy-start.7
  0.6 0.7 and_select_fusion.3
  1.3 0.7 convert_bitcast_fusion.fluid_ref
  2.0 0.1 fusion
  2.1 0.2 reduce_window_sum.11
  2.3 0.2 select_reduce_fusion.3
  2.4 0.7 fusion.3
  3.1 0.2 select_reduce_fusion.1
  3.3 0.1 convert_element_type.30
  3.4 0.0 copy-start.2
  3.4 1.9 copy-done.2
  5.3 0.0 copy-start.3
  5.3 1.2 copy-done.3
  6.5 0.0 copy-start.4
  6.5 0.0 copy-start.8
  6.5 61.3 %brick_exchange.1 = (f32[8,24,3,16,128]{4,3,2,1,0:T(8,128)S(1)}, f32[8,72,128]{2,1,0:T(8,128)S(1)}) custom-call(s32[192]{0:T(256)S(1)} %get-tuple-element.11.src_ref, f32[8,8,128]{2,1,0:T(8,128)S(1)} %pad.4.ids_ref, f32[128,3,16,128]{3,2,1,0:T(8,128)S(1)} %bitcast.20, f32[128,16,128]{2,1,0:T(8,128)S(1)} %bitcast.21), custom_call_target="tpu_custom_call" | custom-call | tf_op jit(solution)/shard_map/brick_exchange/pallas_call | solution.py:181
  67.8 0.0 copy-start
  67.8 2.1 %copy-done = f32[8,24,3,16,128]{4,3,2,1,0:T(8,128)} copy-done((f32[8,24,3,16,128]{4,3,2,1,0:T(8,128)}, f32[8,24,3,16,128]{4,3,2,1,0:T(8,128)S(1)}, u32[]{:S(2)}) %copy-start) | copy-done | bytes 4718616
  69.9 0.1 eq.54
  70.0 0.1 select_reduce_fusion
  70.2 0.0 copy-done.7
  70.2 0.0 copy-done.4
  70.2 0.0 copy-done.8
  70.2 0.0 copy-done.9
  70.2 0.0 copy-done.10
  70.2 0.0 copy-start.1
  70.2 2.2 %copy-done.1 = bf16[2,1024,1024]{2,1,0:T(8,128)(2,1)S(1)} copy-done((bf16[2,1024,1024]{2,1,0:T(8,128)(2,1)S(1)}, bf16[2,1024,1024]{2,1,0:T(8,128)(2,1)}, u32[]{:S(2)}) %copy-start.1) | copy-done | bytes 4194328
  72.4 110.8 %pressure_solver.1 = (f32[1,256,1024]{2,1,0:T(8,128)S(1)}, f32[1,256,1024]{2,1,0:T(8,128)S(1)}) custom-call(s32[128]{0:T(128)S(1)} %get-tuple-element.13.from_ref, s32[128]{0:T(128)S(1)} %get-tuple-element.12.place_ref, f32[128]{0:T(128)S(1)} %convert_bitcast_fusion.fluid_ref, f32[8,24,3,16,128]{4,3,2,1,0:T(8,128)} %copy-done, ...), custom_call_target="tpu_custom_call" | custom-call | tf_op jit(solution)/shard_map/pressure_solver/pallas_call | solution.py:652
  183.3 0.0 copy-start.5
  183.3 1.0 copy-done.5
  184.2 1.0 copy-done.6
  185.3 3.7 %deliver.1 = (f32[1,256,1024]{2,1,0:T(8,128)}, f32[1,256,1024]{2,1,0:T(8,128)}) custom-call(f32[1,256,1024]{2,1,0:T(8,128)} %copy-done.5, f32[1,256,1024]{2,1,0:T(8,128)} %copy-done.6), custom_call_target="tpu_custom_call" | custom-call | tf_op jit(solution)/shard_map/deliver/pallas_call | solution.py:707
  (8 shorter events, 0.1 us)
Async XLA Ops:
  0.6 69.5 %copy-start.7 = (f32[4,2,8,1024]{3,2,1,0:T(8,128)S(1)}, f32[4,2,8,1024]{3,2,1,0:T(8,128)}, u32[]{:S(2)}) copy-start(f32[4,2,8,1024]{3,2,1,0:T(8,128)} %constant.75.clone.couple_ref) | copy-start | bytes 786436
  3.4 1.9 %copy-start.2 = (f32[1,128,3,16,128]{4,3,2,1,0:T(8,128)S(1)}, f32[1,128,3,16,128]{4,3,2,1,0:T(8,128)}, u32[]{:S(2)}) copy-start(f32[1,128,3,16,128]{4,3,2,1,0:T(8,128)} %param.11) | copy-start | bytes 9437188
  5.3 1.2 copy-start.3
  6.5 63.7 %copy-start.4 = (f32[256,1024]{1,0:T(8,128)S(1)}, f32[256,1024]{1,0:T(8,128)}, u32[]{:S(2)}) copy-start(f32[256,1024]{1,0:T(8,128)} %constant.73.clone.inverse_ref) | copy-start | bytes 3145732
  6.5 63.7 %copy-start.8 = (f32[256,256]{1,0:T(8,128)S(1)}, f32[256,256]{1,0:T(8,128)}, u32[]{:S(2)}) copy-start(f32[256,256]{1,0:T(8,128)} %constant.74.clone.ends_ref) | copy-start | bytes 786436
  6.5 63.7 %copy-start.9 = (bf16[2,256,256]{2,1,0:T(8,128)(2,1)S(1)}, bf16[2,256,256]{2,1,0:T(8,128)(2,1)}, u32[]{:S(2)}) copy-start(bf16[2,256,256]{2,1,0:T(8,128)(2,1)} %constant.72.clone.table_xt) | copy-start | bytes 786436
  6.5 63.7 %copy-start.10 = (bf16[2,256,256]{2,1,0:T(8,128)(2,1)S(1)}, bf16[2,256,256]{2,1,0:T(8,128)(2,1)}, u32[]{:S(2)}) copy-start(bf16[2,256,256]{2,1,0:T(8,128)(2,1)} %constant.71.clone.table_x) | copy-start | bytes 786436
  67.8 2.1 %copy-start = (f32[8,24,3,16,128]{4,3,2,1,0:T(8,128)}, f32[8,24,3,16,128]{4,3,2,1,0:T(8,128)S(1)}, u32[]{:S(2)}) copy-start(f32[8,24,3,16,128]{4,3,2,1,0:T(8,128)S(1)} %get-tuple-element.7.main_ref) | copy-start | bytes 14155780
  70.2 2.2 %copy-start.1 = (bf16[2,1024,1024]{2,1,0:T(8,128)(2,1)S(1)}, bf16[2,1024,1024]{2,1,0:T(8,128)(2,1)}, u32[]{:S(2)}) copy-start(bf16[2,1024,1024]{2,1,0:T(8,128)(2,1)} %constant.69.clone.fwd_hbm) | copy-start | bytes 12582916
  183.3 1.0 copy-start.5
  184.2 1.0 copy-start.6
